TPU v7x, 128 devices: a whole 4x4x4 slice. The times are simulated.
128 devices in a mesh: group: 16 (over y, x), member: 8 (over z, core).
Axes of the slice: x: 4, y: 4, z: 4, core: 2. Of those that a mesh axis runs over, the one named last changes fastest.
Arguments:
- tokens: bfloat16 [16384, 2048], P(('group', 'member')), may hold values from -6 to 6
- grad_out: bfloat16 [16384, 2048], P(('group', 'member')), may hold values from -6 to 6
- expert_ids: int32 [16384, 8], P(('group', 'member')), may hold values from 0 to 127, as said below
- pair_slot: int32 [16384, 8], P(('group', 'member')), may hold values from 0 to 11, as said below
- gate_weights: bfloat16 [16384, 8], P(('group', 'member')), may hold values from 0.049804688 to 1
- weight_gate: bfloat16 [128, 2048, 768], P(('group', 'member')), may hold values from -0.125 to 0.125
- weight_up: bfloat16 [128, 2048, 768], P(('group', 'member')), may hold values from -0.125 to 0.125
- weight_down: bfloat16 [128, 768, 2048], P(('group', 'member')), may hold values from -0.21875 to 0.21875
- saved_gate: bfloat16 [128, 1536, 768], P(('group', 'member')), may hold values from -6 to 6
- saved_up: bfloat16 [128, 1536, 768], P(('group', 'member')), may hold values from -6 to 6
Outputs:
- grad_tokens: bfloat16 [16384, 2048], P(('group', 'member'))
- grad_gates: bfloat16 [16384, 8], P(('group', 'member'))
- grad_weight_gate: bfloat16 [128, 2048, 768], P(('group', 'member'))
- grad_weight_up: bfloat16 [128, 2048, 768], P(('group', 'member'))
- grad_weight_down: bfloat16 [128, 768, 2048], P(('group', 'member'))
Inputs may be any that keep to these rules, and one draw needn't show every extreme that they name: `expert_ids`: each token names 8 distinct experts, two in each of exactly 4 groups, the group of expert e being e // 8. The tokens of one device send at most 48 tokens to one group, and in every draw some group gets exactly 48 from every device. `pair_slot`: among one device's assignments to one expert the slots are distinct and run from 0 to their count less one, in no fixed order of tokens. In every draw some expert gets exactly 12 assignments from every device.
All inputs are finite; a program needn't handle non-finite values.
Results may differ from a plain program's by a relative error of at most 0.012.
Values may be sent and summed in bfloat16 or wider, within the bound.
No kernel may reach another device: no remote copies, remote signals or barrier semaphores. Data moves between devices by JAX's collectives and lax.ppermute only.
A program may use at most 192 MiB of HBM per device.

v0:
```python
import jax
import jax.numpy as jnp
from jax import lax
from jax.experimental import pallas as pl
from jax.experimental.pallas import tpu as pltpu
from jax.sharding import PartitionSpec as P

F32 = jnp.float32
BF16 = jnp.bfloat16
AXES = ("group", "member")
CHUNK = 256
NT = (((1,), (1,)), ((), ()))
VMEM_LIMIT = 56 * 1024 * 1024


def zero_one(mask):
    return jnp.where(mask, 1.0, 0.0).astype(BF16)


def dot(a, b):
    return jnp.dot(a, b, preferred_element_type=F32)


def packed_ids(index):
    pair, q = index >> 3, index & 7
    return pair * 12 + q, pair * 12 + 8 + (q & 3), q < 4


def pack_kernel(dest_ref, x_ref, out_ref):
    rows, toks = out_ref.shape[0], x_ref.shape[0]
    width = x_ref.shape[1]
    half = width // 2
    index = lax.broadcasted_iota(jnp.int32, (rows, toks), 0) + pl.program_id(0) * rows
    id_a, id_b, first = packed_ids(index)
    hit_a = dest_ref[0:1, :] == id_a
    hit_b = dest_ref[0:1, :] == id_b
    for k in range(1, dest_ref.shape[0]):
        d = dest_ref[k : k + 1, :]
        hit_a = hit_a | (d == id_a)
        hit_b = hit_b | (d == id_b)
    out_ref[:, :width] = dot(zero_one(hit_a), x_ref[...]).astype(BF16)
    low = dot(zero_one(hit_b & first), x_ref[:, :half])
    high = dot(zero_one(hit_b & jnp.logical_not(first)), x_ref[:, half:])
    out_ref[:, width:] = (low + high).astype(BF16)


def pack(dest_t, x, packed_rows):
    toks, width = x.shape
    return pl.pallas_call(
        pack_kernel,
        grid=(packed_rows // CHUNK,),
        in_specs=[
            pl.BlockSpec(dest_t.shape, lambda i: (0, 0)),
            pl.BlockSpec(x.shape, lambda i: (0, 0)),
        ],
        out_specs=pl.BlockSpec((CHUNK, width * 3 // 2), lambda i: (i, 0)),
        out_shape=jax.ShapeDtypeStruct((packed_rows, width * 3 // 2), BF16),
        compiler_params=pltpu.CompilerParams(vmem_limit_bytes=VMEM_LIMIT),
        cost_estimate=pl.CostEstimate(
            flops=2 * packed_rows * toks * width * 2,
            bytes_accessed=packed_rows * width * 3,
            transcendentals=0,
        ),
    )(dest_t, x)


def sort_kernel(a_ref, b_ref, out_a, out_b):
    rows = a_ref.shape[0]
    n = lax.broadcasted_iota(jnp.int32, (rows, rows), 0)
    col = lax.broadcasted_iota(jnp.int32, (rows, rows), 1)
    cut = rows * 2 // 3
    m = n - cut
    source = jnp.where(n < cut, (n >> 3) * 12 + (n & 7), (m >> 2) * 12 + 8 + (m & 3))
    perm = zero_one(col == source)
    out_a[...] = dot(perm, a_ref[...]).astype(BF16)
    out_b[...] = dot(perm, b_ref[...]).astype(BF16)


def sort_rows(a, b):
    rows, width = a.shape
    step = CHUNK * 3 // 2
    spec = pl.BlockSpec((step, width), lambda i: (i, 0))
    return pl.pallas_call(
        sort_kernel,
        grid=(rows // step,),
        in_specs=[spec, spec],
        out_specs=[spec, spec],
        out_shape=[jax.ShapeDtypeStruct((rows, width), BF16)] * 2,
        compiler_params=pltpu.CompilerParams(vmem_limit_bytes=VMEM_LIMIT),
        cost_estimate=pl.CostEstimate(
            flops=4 * rows * step * width, bytes_accessed=rows * width * 8, transcendentals=0
        ),
    )(a, b)


def fold_masks(out_rows, in_rows):
    n = lax.broadcasted_iota(jnp.int32, (out_rows, in_rows), 0)
    p = lax.broadcasted_iota(jnp.int32, (out_rows, in_rows), 1)
    low = (n >> 2) * 8 + (n & 3)
    return zero_one(p == low), zero_one(p == low + 4)


def unpack_into(packed_ref, rows_ref):
    packed = packed_ref.shape[0]
    width = rows_ref.shape[1]
    half = width // 2
    rows_ref[:packed, :] = packed_ref[:, :width]
    low, high = fold_masks(packed // 2, packed)
    rest = packed_ref[:, width:]
    rows_ref[packed:, :half] = dot(low, rest).astype(BF16)
    rows_ref[packed:, half:] = dot(high, rest).astype(BF16)


def unpack(packed):
    total, wide = packed.shape
    width = wide * 2 // 3
    return pl.pallas_call(
        unpack_into,
        grid=(total // CHUNK,),
        in_specs=[pl.BlockSpec((CHUNK, wide), lambda i: (i, 0))],
        out_specs=pl.BlockSpec((CHUNK * 3 // 2, width), lambda i: (i, 0)),
        out_shape=jax.ShapeDtypeStruct((total * 3 // 2, width), BF16),
        compiler_params=pltpu.CompilerParams(vmem_limit_bytes=VMEM_LIMIT),
        cost_estimate=pl.CostEstimate(
            flops=total * CHUNK * width * 2, bytes_accessed=total * wide * 4, transcendentals=0
        ),
    )(packed)


def expert_kernel(
    packed_ref,
    gate_ref,
    a_ref,
    b_ref,
    wg_ref,
    wu_ref,
    wd_ref,
    back_ref,
    rows_ref,
    hidden_ref,
    pregate_ref,
    preup_ref,
    slot_gate_ref,
):
    packed = packed_ref.shape[0]
    width = rows_ref.shape[1]
    half = width // 2
    unpack_into(packed_ref, rows_ref)
    back_hidden = lax.dot_general(rows_ref[...], wd_ref[...], NT, preferred_element_type=F32)
    a = a_ref[...].astype(F32)
    b = b_ref[...].astype(F32)
    scale = gate_ref[...]
    sig = jax.nn.sigmoid(a)
    swish = a * sig
    hidden = swish * b
    hidden_ref[...] = (hidden * scale).astype(BF16)
    slot_gate_ref[...] = jnp.sum(hidden * back_hidden, axis=1, keepdims=True)
    hidden_grad = scale * back_hidden
    pregate = (hidden_grad * b * sig * (1.0 + a * (1.0 - sig))).astype(BF16)
    preup = (hidden_grad * swish).astype(BF16)
    pregate_ref[...] = pregate
    preup_ref[...] = preup
    slot_grad = (
        lax.dot_general(pregate, wg_ref[...], NT, preferred_element_type=F32)
        + lax.dot_general(preup, wu_ref[...], NT, preferred_element_type=F32)
    ).astype(BF16)
    back_ref[:, :width] = slot_grad[:packed, :]
    p = lax.broadcasted_iota(jnp.int32, (packed, packed // 2), 0)
    n = lax.broadcasted_iota(jnp.int32, (packed, packed // 2), 1)
    same = n == (p >> 3) * 4 + (p & 3)
    first = (p & 7) < 4
    rest = slot_grad[packed:, :]
    back_ref[:, width:] = (
        dot(zero_one(same & first), rest[:, :half])
        + dot(zero_one(same & jnp.logical_not(first)), rest[:, half:])
    ).astype(BF16)


def expert(packed, gates, a, b, weight_gate, weight_up, weight_down):
    total, wide = packed.shape
    rows = total * 3 // 2
    hidden_units, width = weight_down.shape
    step = CHUNK * 3 // 2
    narrow = pl.BlockSpec((step, hidden_units), lambda i: (i, 0))
    column = pl.BlockSpec((step, 1), lambda i: (i, 0))
    packed_spec = pl.BlockSpec((CHUNK, wide), lambda i: (i, 0))
    return pl.pallas_call(
        expert_kernel,
        grid=(total // CHUNK,),
        in_specs=[
            packed_spec,
            column,
            narrow,
            narrow,
            pl.BlockSpec(weight_gate.shape, lambda i: (0, 0)),
            pl.BlockSpec(weight_up.shape, lambda i: (0, 0)),
            pl.BlockSpec(weight_down.shape, lambda i: (0, 0)),
        ],
        out_specs=[
            packed_spec,
            pl.BlockSpec((step, width), lambda i: (i, 0)),
            narrow,
            narrow,
            narrow,
            column,
        ],
        out_shape=[
            jax.ShapeDtypeStruct((total, wide), BF16),
            jax.ShapeDtypeStruct((rows, width), BF16),
            jax.ShapeDtypeStruct((rows, hidden_units), BF16),
            jax.ShapeDtypeStruct((rows, hidden_units), BF16),
            jax.ShapeDtypeStruct((rows, hidden_units), BF16),
            jax.ShapeDtypeStruct((rows, 1), F32),
        ],
        compiler_params=pltpu.CompilerParams(vmem_limit_bytes=VMEM_LIMIT),
        cost_estimate=pl.CostEstimate(
            flops=6 * rows * width * hidden_units,
            bytes_accessed=total * wide * 6,
            transcendentals=rows * hidden_units,
        ),
    )(packed, gates, a, b, weight_gate, weight_up, weight_down)


def combine_kernel(dest_ref, packed_ref, out_ref, acc_ref):
    step = pl.program_id(0)
    toks, width = out_ref.shape
    half = width // 2
    rows = packed_ref.shape[0]
    index = lax.broadcasted_iota(jnp.int32, (toks, rows), 1) + step * rows
    id_a, id_b, first = packed_ids(index)
    hit_a = dest_ref[:, 0:1] == id_a
    hit_b = dest_ref[:, 0:1] == id_b
    for k in range(1, dest_ref.shape[1]):
        d = dest_ref[:, k : k + 1]
        hit_a = hit_a | (d == id_a)
        hit_b = hit_b | (d == id_b)
    rest = packed_ref[:, width:]
    one_a = zero_one(hit_a)

    @pl.when(step == 0)
    def _():
        acc_ref[...] = jnp.zeros_like(acc_ref)

    acc_ref[:, :half] += dot(one_a, packed_ref[:, :half]) + dot(zero_one(hit_b & first), rest)
    acc_ref[:, half:] += dot(one_a, packed_ref[:, half:width]) + dot(
        zero_one(hit_b & jnp.logical_not(first)), rest
    )

    @pl.when(step == pl.num_programs(0) - 1)
    def _():
        out_ref[...] = acc_ref[...].astype(BF16)


def combine(dest, packed, toks):
    total, wide = packed.shape
    width = wide * 2 // 3
    return pl.pallas_call(
        combine_kernel,
        grid=(total // CHUNK,),
        in_specs=[
            pl.BlockSpec(dest.shape, lambda i: (0, 0)),
            pl.BlockSpec((CHUNK, wide), lambda i: (i, 0)),
        ],
        out_specs=pl.BlockSpec((toks, width), lambda i: (0, 0)),
        out_shape=jax.ShapeDtypeStruct((toks, width), BF16),
        scratch_shapes=[pltpu.VMEM((toks, width), F32)],
        compiler_params=pltpu.CompilerParams(vmem_limit_bytes=VMEM_LIMIT),
        cost_estimate=pl.CostEstimate(
            flops=2 * total * toks * width * 2, bytes_accessed=total * wide * 2, transcendentals=0
        ),
    )(dest, packed)


def exchange(x):
    return lax.all_to_all(x, AXES, split_axis=0, concat_axis=0, tiled=True)


def gather_all(x):
    return lax.all_gather(x, AXES, axis=0, tiled=False)


def sort_pairs(x, experts):
    x = x.reshape(experts * 8 // CHUNK, CHUNK // 8, 12)
    first = x[:, :, :8].reshape(x.shape[0], -1)
    last = x[:, :, 8:].reshape(x.shape[0], -1)
    return jnp.concatenate([first, last], axis=1).reshape(-1)


def unsort_pairs(x, experts):
    chunks = experts * 8 // CHUNK
    x = x.reshape(chunks, -1)
    first = x[:, :CHUNK].reshape(chunks, CHUNK // 8, 8)
    last = x[:, CHUNK:].reshape(chunks, CHUNK // 8, 4)
    return jnp.concatenate([first, last], axis=2).reshape(-1)


def body(
    tokens,
    grad_out,
    expert_ids,
    pair_slot,
    gate_weights,
    weight_gate,
    weight_up,
    weight_down,
    saved_gate,
    saved_up,
):
    experts = lax.axis_size("group") * lax.axis_size("member")
    me = lax.axis_index("group") * lax.axis_size("member") + lax.axis_index("member")
    toks, width = tokens.shape
    route_count = expert_ids.shape[1]
    pair_rows = saved_gate.shape[1] // experts
    packed_rows = experts * 8
    dest = expert_ids * pair_rows + pair_slot
    dest_t = expert_ids.T * pair_rows + pair_slot.T

    sent_grads = pack(dest_t, grad_out, packed_rows)
    here_grads = exchange(sent_grads)
    here_tokens = exchange(pack(dest_t, tokens, packed_rows))

    all_dest = gather_all(dest_t).reshape(experts, 1, -1)
    all_gates = gather_all(gate_weights.T).reshape(experts, 1, -1)
    wanted = (me * pair_rows + jnp.arange(pair_rows, dtype=jnp.int32))[None, :, None]
    gates = jnp.sum(jnp.where(all_dest == wanted, all_gates.astype(F32), 0.0), axis=2)
    gates = sort_pairs(gates, experts)[:, None]
    a, b = sort_rows(saved_gate[0], saved_up[0])

    back, grad_rows, hidden, pregate, preup, slot_gate = expert(
        here_grads, gates, a, b, weight_gate[0], weight_up[0], weight_down[0]
    )
    back_packed = exchange(back)

    slot_gate = unsort_pairs(slot_gate.astype(BF16)[:, 0], experts)
    all_slot_gates = gather_all(slot_gate)
    mine = lax.dynamic_slice(all_slot_gates, (0, me * pair_rows), (experts, pair_rows))
    grad_gates = jnp.take(mine.reshape(-1), dest.reshape(-1), axis=0, mode="clip")

    token_rows = unpack(here_tokens)
    over_rows = (((0,), (0,)), ((), ()))
    down_total = lax.dot_general(hidden, grad_rows, over_rows, preferred_element_type=F32)
    gate_total = lax.dot_general(token_rows, pregate, over_rows, preferred_element_type=F32)
    up_total = lax.dot_general(token_rows, preup, over_rows, preferred_element_type=F32)

    grad_tokens = combine(dest, back_packed, toks)
    return (
        grad_tokens,
        grad_gates.reshape(toks, route_count),
        gate_total[None].astype(BF16),
        up_total[None].astype(BF16),
        down_total[None].astype(BF16),
    )


def solution(mesh):
    rows = P(AXES, None)
    blocks = P(AXES, None, None)
    return jax.shard_map(
        body,
        mesh=mesh,
        in_specs=(rows,) * 5 + (blocks,) * 5,
        out_specs=(rows, rows, blocks, blocks, blocks),
        check_vma=False,
    )
```

profile of v0, /device:TPU:1, one launch (start us, length us, event | category | flops | bytes accessed | tf_op | source)
XLA Modules:
  0.0 432.3 jit_solution(15636918839456724079)
XLA Ops:
  0.6 1.3 multiply_add_fusion
  1.9 5.8 %shard_map.137 = bf16[1024,3072]{1,0:T(8,128)(2,1)} custom-call(s32[8,128]{1,0:T(8,128)} %bitcast.38, bf16[128,2048]{1,0:T(8,128)(2,1)} %x_ref.2), custom_call_target="tpu_custom_call" | custom-call | flops 1073741824 | bytes 6291456 | tf_op jit(solution)/shard_map/pallas_call | solution.py:49
  7.7 11.9 %all-to-all-start = ((bf16[128,8,3072]{2,1,0:T(8,128)(2,1)}), bf16[128,8,3072]{2,1,0:T(8,128)(2,1)}, u32[]{:S(2)}, u32[]{:S(2)}) async-start(bf16[128,8,3072]{2,1,0:T(8,128)(2,1)} %bitcast.33), calls=%async_computation | async-start | bytes 12582912 | tf_op jit(solution)/shard_map/all_to_all | solution.py:275
  19.6 5.9 %shard_map.141 = bf16[1024,3072]{1,0:T(8,128)(2,1)} custom-call(s32[8,128]{1,0:T(8,128)} %bitcast.39, bf16[128,2048]{1,0:T(8,128)(2,1)} %x_ref.3), custom_call_target="tpu_custom_call" | custom-call | flops 1073741824 | bytes 6291456 | tf_op jit(solution)/shard_map/pallas_call | solution.py:49
  25.5 71.0 %all-to-all-done = bf16[128,8,3072]{2,1,0:T(8,128)(2,1)} async-done(((bf16[128,8,3072]{2,1,0:T(8,128)(2,1)}), bf16[128,8,3072]{2,1,0:T(8,128)(2,1)}, u32[]{:S(2)}, u32[]{:S(2)}) %all-to-all-start) | async-done | bytes 6291488 | tf_op jit(solution)/shard_map/all_to_all | solution.py:275
  96.5 8.6 %all-to-all-start.2 = ((bf16[128,8,3072]{2,1,0:T(8,128)(2,1)}), bf16[128,8,3072]{2,1,0:T(8,128)(2,1)}, u32[]{:S(2)}, u32[]{:S(2)}) async-start(bf16[128,8,3072]{2,1,0:T(8,128)(2,1)} %bitcast.32), calls=%async_computation.2 | async-start | bytes 12582912 | tf_op jit(solution)/shard_map/all_to_all | solution.py:275
  105.1 104.5 %all-gather = s32[1024,128]{1,0:T(8,128)S(1)} all-gather(s32[8,128]{1,0:T(8,128)S(1)} %bitcast.40), channel_id=2, replica_groups=mesh['group'=16,'member'=8] {'group','member'}, dimensions={0}, use_global_device_ids=true | all-gather | bytes 528384 | tf_op jit(solution)/shard_map/all_gather | solution.py:279
  209.7 33.3 %all-gather.1 = bf16[1024,128]{1,0:T(8,128)(2,1)S(1)} all-gather(bf16[8,128]{1,0:T(8,128)(2,1)S(1)} %bitcast.42), channel_id=3, replica_groups=mesh['group'=16,'member'=8] {'group','member'}, dimensions={0}, use_global_device_ids=true | all-gather | bytes 264192 | tf_op jit(solution)/shard_map/all_gather | solution.py:279
  243.1 0.7 select_reduce_fusion
  244.3 1.2 copy.35
  245.5 6.0 %shard_map.138 = (bf16[1536,768]{1,0:T(8,128)(2,1)}, bf16[1536,768]{1,0:T(8,128)(2,1)}) custom-call(bf16[1536,768]{1,0:T(8,128)(2,1)} %bitcast.46, bf16[1536,768]{1,0:T(8,128)(2,1)} %bitcast.47), custom_call_target="tpu_custom_call" | custom-call | flops 1811939328 | bytes 9437184 | tf_op jit(solution)/shard_map/pallas_call | solution.py:83
  251.5 28.8 %shard_map.139 = (bf16[1024,3072]{1,0:T(8,128)(2,1)}, bf16[1536,2048]{1,0:T(8,128)(2,1)}, bf16[1536,768]{1,0:T(8,128)(2,1)}, bf16[1536,768]{1,0:T(8,128)(2,1)}, ...) custom-call(bf16[1024,3072]{1,0:T(8,128)(2,1)} %bitcast.2.packed_ref, f32[1536,1]{1,0:T(8,128)} %bitcast.35, ...), custom_call_target="tpu_custom_call" | custom-call | flops 14495514624 | bytes 18874368 | tf_op jit(solution)/shard_map/pallas_call | solution.py:187
  280.3 5.1 %all-to-all-start.1 = ((bf16[128,8,3072]{2,1,0:T(8,128)(2,1)}), bf16[128,8,3072]{2,1,0:T(8,128)(2,1)}, u32[]{:S(2)}, u32[]{:S(2)}) async-start(bf16[128,8,3072]{2,1,0:T(8,128)(2,1)} %bitcast.34), calls=%async_computation.1 | async-start | bytes 12582912 | tf_op jit(solution)/shard_map/all_to_all | solution.py:275
  285.6 0.3 convert_reduce_fusion
  286.4 102.3 %all-gather.2 = bf16[128,1,1536]{2,1,0:T(2,128)(2,1)S(1)} all-gather(bf16[1,1,1536]{2,1,0:T(2,128)(2,1)S(1)} %reshape.80), channel_id=1, replica_groups=mesh['group'=16,'member'=8] {'group','member'}, dimensions={0}, use_global_device_ids=true | all-gather | bytes 396288 | tf_op jit(solution)/shard_map/all_gather | solution.py:279
  388.7 0.3 dynamic-slice_reduce_fusion
  388.9 0.1 reshape.63
  389.1 6.8 %gather_fusion = bf16[1024]{0:T(1024)(128)(2,1)S(1)} fusion(bf16[1536]{0:T(1024)(128)(2,1)S(1)} %reshape.63, s32[1024]{0:T(1024)S(1)} %broadcast_clamp_fusion), kind=kCustom, calls=%fused_computation | custom fusion | bytes 8192 | tf_op jit(solution)/shard_map/jit(_take)/gather | solution.py:337
  396.0 0.7 copy.32
  396.6 6.5 %shard_map.142 = bf16[1536,2048]{1,0:T(8,128)(2,1)} custom-call(bf16[1024,3072]{1,0:T(8,128)(2,1)} %bitcast.12.packed_ref), custom_call_target="tpu_custom_call" | custom-call | flops 1073741824 | bytes 12582912 | tf_op jit(solution)/shard_map/pallas_call | solution.py:117
  403.1 9.7 %fusion = bf16[1,2048,768]{2,1,0:T(8,128)(2,1)} fusion(bf16[1536,2048]{1,0:T(8,128)(2,1)} %shard_map.142, bf16[1536,768]{1,0:T(8,128)(2,1)S(1)} %copy-done.7), kind=kOutput, calls=%fused_computation.5 | convolution fusion | flops 4833411072 | bytes 11796480 | tf_op jit(solution)/shard_map/dot_general | solution.py:342
  412.9 6.5 %fusion.1 = bf16[1,2048,768]{2,1,0:T(8,128)(2,1)} fusion(bf16[1536,2048]{1,0:T(8,128)(2,1)S(1)} %copy-done, bf16[1536,768]{1,0:T(8,128)(2,1)S(1)} %copy-done.6), kind=kOutput, calls=%fused_computation.6 | convolution fusion | flops 4833411072 | bytes 11796480 | tf_op jit(solution)/shard_map/dot_general | solution.py:343
  419.4 6.5 %fusion.2 = bf16[1,768,2048]{2,1,0:T(8,128)(2,1)} fusion(bf16[1536,768]{1,0:T(8,128)(2,1)S(1)} %copy-done.5, bf16[1536,2048]{1,0:T(8,128)(2,1)S(1)} %bitcast.49), kind=kOutput, calls=%fused_computation.7 | convolution fusion | flops 4833411072 | bytes 11796480 | tf_op jit(solution)/shard_map/dot_general | solution.py:341
  425.9 6.4 %shard_map.140 = bf16[128,2048]{1,0:T(8,128)(2,1)} custom-call(s32[128,8]{1,0:T(8,128)} %copy-done.2, bf16[1024,3072]{1,0:T(8,128)(2,1)} %bitcast.10.packed_ref), custom_call_target="tpu_custom_call" | custom-call | flops 1073741824 | bytes 6291456 | tf_op jit(solution)/shard_map/pallas_call | solution.py:257
  (43 shorter events, 1.4 us)
Async XLA Ops:
  7.7 88.7 %all-to-all-start = ((bf16[128,8,3072]{2,1,0:T(8,128)(2,1)}), bf16[128,8,3072]{2,1,0:T(8,128)(2,1)}, u32[]{:S(2)}, u32[]{:S(2)}) async-start(bf16[128,8,3072]{2,1,0:T(8,128)(2,1)} %bitcast.33), calls=%async_computation | async-start | bytes 12582912 | tf_op jit(solution)/shard_map/all_to_all | solution.py:275
  96.5 8.6 %copy-start.3 = (s32[128,8]{0,1:T(8,128)S(1)}, s32[128,8]{0,1:T(8,128)}, u32[]{:S(2)}) copy-start(s32[128,8]{0,1:T(8,128)} %multiply_add_fusion) | copy-start | bytes 12292
  96.5 113.2 %copy-start.4 = (bf16[128,8]{0,1:T(8,128)(2,1)S(1)}, bf16[128,8]{0,1:T(8,128)(2,1)}, u32[]{:S(2)}) copy-start(bf16[128,8]{0,1:T(8,128)(2,1)} %param.14) | copy-start | bytes 6148
  96.5 183.8 %all-to-all-start.2 = ((bf16[128,8,3072]{2,1,0:T(8,128)(2,1)}), bf16[128,8,3072]{2,1,0:T(8,128)(2,1)}, u32[]{:S(2)}, u32[]{:S(2)}) async-start(bf16[128,8,3072]{2,1,0:T(8,128)(2,1)} %bitcast.32), calls=%async_computation.2 | async-start | bytes 12582912 | tf_op jit(solution)/shard_map/all_to_all | solution.py:275
  280.3 5.3 %copy-start.1 = (f32[1536,1]{1,0:T(8,128)S(1)}, f32[1536,1]{1,0:T(8,128)}, u32[]{:S(2)}) copy-start(f32[1536,1]{1,0:T(8,128)} %get-tuple-element.16) | copy-start | bytes 18436
  280.3 145.6 %all-to-all-start.1 = ((bf16[128,8,3072]{2,1,0:T(8,128)(2,1)}), bf16[128,8,3072]{2,1,0:T(8,128)(2,1)}, u32[]{:S(2)}, u32[]{:S(2)}) async-start(bf16[128,8,3072]{2,1,0:T(8,128)(2,1)} %bitcast.34), calls=%async_computation.1 | async-start | bytes 12582912 | tf_op jit(solution)/shard_map/all_to_all | solution.py:275
  285.5 117.6 %copy-start.2 = (s32[128,8]{1,0:T(8,128)}, s32[128,8]{1,0:T(8,128)S(1)}, u32[]{:S(2)}) copy-start(s32[128,8]{1,0:T(8,128)S(1)} %copy.30.dest_ref) | copy-start | bytes 12292
  396.6 6.5 %copy-start.7 = (bf16[1536,768]{1,0:T(8,128)(2,1)S(1)}, bf16[1536,768]{1,0:T(8,128)(2,1)}, u32[]{:S(2)}) copy-start(bf16[1536,768]{1,0:T(8,128)(2,1)} %get-tuple-element.17) | copy-start | bytes 7077892
  403.1 9.7 %copy-start = (bf16[1536,2048]{1,0:T(8,128)(2,1)S(1)}, bf16[1536,2048]{1,0:T(8,128)(2,1)}, u32[]{:S(2)}) copy-start(bf16[1536,2048]{1,0:T(8,128)(2,1)} %shard_map.142) | copy-start | bytes 18874372
  403.1 9.7 %copy-start.6 = (bf16[1536,768]{1,0:T(8,128)(2,1)S(1)}, bf16[1536,768]{1,0:T(8,128)(2,1)}, u32[]{:S(2)}) copy-start(bf16[1536,768]{1,0:T(8,128)(2,1)} %get-tuple-element.18) | copy-start | bytes 7077892
  403.1 16.3 %slice-start = ((s8[6291456]{0:T(1024)(128)(4,1)}), s8[4194304]{0:T(1024)(128)(4,1)S(1)}, s32[]{:S(2)}) async-start(s8[6291456]{0:T(1024)(128)(4,1)} %bitcast.48), calls=%async_computation.3 | async-start | bytes 8388608
  412.9 6.6 %slice-start.1 = ((s8[6291456]{0:T(1024)(128)(4,1)}), s8[2097152]{0:T(1024)(128)(4,1)S(1)}, s32[]{:S(2)}) async-start(s8[6291456]{0:T(1024)(128)(4,1)} %bitcast.48), calls=%async_computation.4 | async-start | bytes 4194304
  412.9 6.6 %copy-start.5 = (bf16[1536,768]{1,0:T(8,128)(2,1)S(1)}, bf16[1536,768]{1,0:T(8,128)(2,1)}, u32[]{:S(2)}) copy-start(bf16[1536,768]{1,0:T(8,128)(2,1)} %get-tuple-element.19) | copy-start | bytes 7077892
where the time goes:
time: 433 us; the launch traced here: 432 us
  blocking collectives  240 us (55%)
  waiting for transfers between devices  71 us (16%)
  Pallas kernels  59.4 us (14%)
  starting transfers between devices  25.6 us (6%)
  matrix products  22.7 us (5%)
  local copies, waits for them, and re-layouts  10.4 us (2%)
    all_gather x3, blocking collectives, gather_all(): return lax.all_gather(x, AXES, axis=0, tiled=False)  240 us
    all_to_all x3, waiting for transfers between devices, exchange(): return lax.all_to_all(x, AXES, split_axis=0, concat_axis=0, tiled=True)  71 us
    pallas_call x1, Pallas kernels, expert(): pl.pallas_call(expert_kernel, grid=(total // CHUNK,), in_specs=[packed_sp...  28.8 us
    all_to_all x3, starting transfers between devices, exchange(): return lax.all_to_all(x, AXES, split_axis=0, concat_axis=0, tiled=True)  25.6 us
    pallas_call x2, Pallas kernels, pack(): pl.pallas_call(pack_kernel, grid=(packed_rows // CHUNK,), in_specs=[pl.Bl...  11.7 us
    dot_general x1, matrix products, body(): lax.dot_general(token_rows, pregate, over_rows, preferred_element_type=F32)  9.71 us
  transfers between devices with their start and end apart: 3, of which 1 were waited for; matrix products, arithmetic and copies ran while one was open for 8% of the time, Pallas kernels for 11%

commit v1 on v0

--- a/solution.py
+++ b/solution.py
@@ -12,6 +12,8 @@
 NT = (((1,), (1,)), ((), ()))
 VMEM_LIMIT = 56 * 1024 * 1024
 
+EXTRA = 128
+
 
 def zero_one(mask):
     return jnp.where(mask, 1.0, 0.0).astype(BF16)
@@ -26,7 +28,12 @@
     return pair * 12 + q, pair * 12 + 8 + (q & 3), q < 4
 
 
-def pack_kernel(dest_ref, x_ref, out_ref):
+def side_by_side(a, b):
+    lane = lax.broadcasted_iota(jnp.int32, (a.shape[0], EXTRA), 1)
+    return jnp.where(lane < EXTRA // 2, a, b).astype(BF16)
+
+
+def pack_kernel(dest_ref, gate_ref, x_ref, out_ref):
     rows, toks = out_ref.shape[0], x_ref.shape[0]
     width = x_ref.shape[1]
     half = width // 2
@@ -41,27 +48,40 @@
     out_ref[:, :width] = dot(zero_one(hit_a), x_ref[...]).astype(BF16)
     low = dot(zero_one(hit_b & first), x_ref[:, :half])
     high = dot(zero_one(hit_b & jnp.logical_not(first)), x_ref[:, half:])
-    out_ref[:, width:] = (low + high).astype(BF16)
-
-
-def pack(dest_t, x, packed_rows):
+    out_ref[:, width : width + half] = (low + high).astype(BF16)
+    if out_ref.shape[1] > width + half:
+        gate_a = jnp.zeros((rows, toks), F32)
+        gate_b = jnp.zeros((rows, toks), F32)
+        for k in range(dest_ref.shape[0]):
+            d = dest_ref[k : k + 1, :]
+            g = gate_ref[k : k + 1, :]
+            gate_a = jnp.where(d == id_a, g, gate_a)
+            gate_b = jnp.where(d == id_b, g, gate_b)
+        out_ref[:, width + half :] = side_by_side(
+            jnp.sum(gate_a, axis=1, keepdims=True), jnp.sum(gate_b, axis=1, keepdims=True)
+        )
+
+
+def pack(dest_t, gates_t, x, packed_rows, extra):
     toks, width = x.shape
+    wide = width * 3 // 2 + extra
     return pl.pallas_call(
         pack_kernel,
         grid=(packed_rows // CHUNK,),
         in_specs=[
             pl.BlockSpec(dest_t.shape, lambda i: (0, 0)),
+            pl.BlockSpec(gates_t.shape, lambda i: (0, 0)),
             pl.BlockSpec(x.shape, lambda i: (0, 0)),
         ],
-        out_specs=pl.BlockSpec((CHUNK, width * 3 // 2), lambda i: (i, 0)),
-        out_shape=jax.ShapeDtypeStruct((packed_rows, width * 3 // 2), BF16),
+        out_specs=pl.BlockSpec((CHUNK, wide), lambda i: (i, 0)),
+        out_shape=jax.ShapeDtypeStruct((packed_rows, wide), BF16),
         compiler_params=pltpu.CompilerParams(vmem_limit_bytes=VMEM_LIMIT),
         cost_estimate=pl.CostEstimate(
             flops=2 * packed_rows * toks * width * 2,
             bytes_accessed=packed_rows * width * 3,
             transcendentals=0,
         ),
-    )(dest_t, x)
+    )(dest_t, gates_t, x)
 
 
 def sort_kernel(a_ref, b_ref, out_a, out_b):
@@ -106,7 +126,7 @@
     half = width // 2
     rows_ref[:packed, :] = packed_ref[:, :width]
     low, high = fold_masks(packed // 2, packed)
-    rest = packed_ref[:, width:]
+    rest = packed_ref[:, width : width + half]
     rows_ref[packed:, :half] = dot(low, rest).astype(BF16)
     rows_ref[packed:, half:] = dot(high, rest).astype(BF16)
 
@@ -129,7 +149,6 @@
 
 def expert_kernel(
     packed_ref,
-    gate_ref,
     a_ref,
     b_ref,
     wg_ref,
@@ -140,7 +159,7 @@
     hidden_ref,
     pregate_ref,
     preup_ref,
-    slot_gate_ref,
+    scale_ref,
 ):
     packed = packed_ref.shape[0]
     width = rows_ref.shape[1]
@@ -149,12 +168,15 @@
     back_hidden = lax.dot_general(rows_ref[...], wd_ref[...], NT, preferred_element_type=F32)
     a = a_ref[...].astype(F32)
     b = b_ref[...].astype(F32)
-    scale = gate_ref[...]
+    extra = packed_ref[:, width + half :]
+    scale_ref[:packed, :] = extra[:, :1].astype(F32)
+    scale_ref[packed:, :] = dot(fold_masks(packed // 2, packed)[0], extra)[:, EXTRA // 2 : EXTRA // 2 + 1]
+    scale = scale_ref[...]
     sig = jax.nn.sigmoid(a)
     swish = a * sig
     hidden = swish * b
     hidden_ref[...] = (hidden * scale).astype(BF16)
-    slot_gate_ref[...] = jnp.sum(hidden * back_hidden, axis=1, keepdims=True)
+    slot_gate = jnp.sum(hidden * back_hidden, axis=1, keepdims=True).astype(BF16)
     hidden_grad = scale * back_hidden
     pregate = (hidden_grad * b * sig * (1.0 + a * (1.0 - sig))).astype(BF16)
     preup = (hidden_grad * swish).astype(BF16)
@@ -170,26 +192,28 @@
     same = n == (p >> 3) * 4 + (p & 3)
     first = (p & 7) < 4
     rest = slot_grad[packed:, :]
-    back_ref[:, width:] = (
+    back_ref[:, width : width + half] = (
         dot(zero_one(same & first), rest[:, :half])
         + dot(zero_one(same & jnp.logical_not(first)), rest[:, half:])
     ).astype(BF16)
-
-
-def expert(packed, gates, a, b, weight_gate, weight_up, weight_down):
+    last = jnp.broadcast_to(slot_gate[packed:, :], (packed // 2, EXTRA))
+    back_ref[:, width + half :] = side_by_side(
+        slot_gate[:packed, :].astype(F32), dot(zero_one(same), last)
+    )
+
+
+def expert(packed, a, b, weight_gate, weight_up, weight_down):
     total, wide = packed.shape
-    rows = total * 3 // 2
+    rows = a.shape[0]
     hidden_units, width = weight_down.shape
     step = CHUNK * 3 // 2
     narrow = pl.BlockSpec((step, hidden_units), lambda i: (i, 0))
-    column = pl.BlockSpec((step, 1), lambda i: (i, 0))
     packed_spec = pl.BlockSpec((CHUNK, wide), lambda i: (i, 0))
     return pl.pallas_call(
         expert_kernel,
         grid=(total // CHUNK,),
         in_specs=[
             packed_spec,
-            column,
             narrow,
             narrow,
             pl.BlockSpec(weight_gate.shape, lambda i: (0, 0)),
@@ -202,7 +226,6 @@
             narrow,
             narrow,
             narrow,
-            column,
         ],
         out_shape=[
             jax.ShapeDtypeStruct((total, wide), BF16),
@@ -210,36 +233,51 @@
             jax.ShapeDtypeStruct((rows, hidden_units), BF16),
             jax.ShapeDtypeStruct((rows, hidden_units), BF16),
             jax.ShapeDtypeStruct((rows, hidden_units), BF16),
-            jax.ShapeDtypeStruct((rows, 1), F32),
-        ],
+        ],
+        scratch_shapes=[pltpu.VMEM((step, 1), F32)],
         compiler_params=pltpu.CompilerParams(vmem_limit_bytes=VMEM_LIMIT),
         cost_estimate=pl.CostEstimate(
             flops=6 * rows * width * hidden_units,
             bytes_accessed=total * wide * 6,
             transcendentals=rows * hidden_units,
         ),
-    )(packed, gates, a, b, weight_gate, weight_up, weight_down)
-
-
-def combine_kernel(dest_ref, packed_ref, out_ref, acc_ref):
+    )(packed, a, b, weight_gate, weight_up, weight_down)
+
+
+def combine_kernel(dest_ref, packed_ref, out_ref, gate_ref, acc_ref, gate_acc_ref):
     step = pl.program_id(0)
     toks, width = out_ref.shape
     half = width // 2
     rows = packed_ref.shape[0]
     index = lax.broadcasted_iota(jnp.int32, (toks, rows), 1) + step * rows
     id_a, id_b, first = packed_ids(index)
-    hit_a = dest_ref[:, 0:1] == id_a
-    hit_b = dest_ref[:, 0:1] == id_b
-    for k in range(1, dest_ref.shape[1]):
-        d = dest_ref[:, k : k + 1]
-        hit_a = hit_a | (d == id_a)
-        hit_b = hit_b | (d == id_b)
-    rest = packed_ref[:, width:]
-    one_a = zero_one(hit_a)
 
     @pl.when(step == 0)
     def _():
         acc_ref[...] = jnp.zeros_like(acc_ref)
+        gate_acc_ref[...] = jnp.zeros_like(gate_acc_ref)
+
+    extra = packed_ref[:, width + half :]
+    lane = lax.broadcasted_iota(jnp.int32, (16, EXTRA), 1)
+    pick = lax.broadcasted_iota(jnp.int32, (16, EXTRA), 0) * (EXTRA // 2)
+    values = lax.dot_general(zero_one(lane == pick), extra, NT, preferred_element_type=F32)
+    value_a = values[0:1, :]
+    value_b = jnp.where(first[:1, :], values[1:2, :], 0.0)
+    column = lax.broadcasted_iota(jnp.int32, gate_acc_ref.shape, 1)
+    hit_a = index < 0
+    hit_b = index < 0
+    gates = gate_acc_ref[...]
+    for k in range(dest_ref.shape[1]):
+        d = dest_ref[:, k : k + 1]
+        here_a = d == id_a
+        here_b = d == id_b
+        hit_a = hit_a | here_a
+        hit_b = hit_b | here_b
+        found = jnp.where(here_a, value_a, jnp.where(here_b, value_b, 0.0))
+        gates += jnp.where(column == k, jnp.sum(found, axis=1, keepdims=True), 0.0)
+    gate_acc_ref[...] = gates
+    rest = packed_ref[:, width : width + half]
+    one_a = zero_one(hit_a)
 
     acc_ref[:, :half] += dot(one_a, packed_ref[:, :half]) + dot(zero_one(hit_b & first), rest)
     acc_ref[:, half:] += dot(one_a, packed_ref[:, half:width]) + dot(
@@ -249,11 +287,12 @@
     @pl.when(step == pl.num_programs(0) - 1)
     def _():
         out_ref[...] = acc_ref[...].astype(BF16)
-
-
-def combine(dest, packed, toks):
+        gate_ref[...] = gates[:, : gate_ref.shape[1]].astype(BF16)
+
+
+def combine(dest, packed, width):
+    toks, routes = dest.shape
     total, wide = packed.shape
-    width = wide * 2 // 3
     return pl.pallas_call(
         combine_kernel,
         grid=(total // CHUNK,),
@@ -261,9 +300,15 @@
             pl.BlockSpec(dest.shape, lambda i: (0, 0)),
             pl.BlockSpec((CHUNK, wide), lambda i: (i, 0)),
         ],
-        out_specs=pl.BlockSpec((toks, width), lambda i: (0, 0)),
-        out_shape=jax.ShapeDtypeStruct((toks, width), BF16),
-        scratch_shapes=[pltpu.VMEM((toks, width), F32)],
+        out_specs=[
+            pl.BlockSpec((toks, width), lambda i: (0, 0)),
+            pl.BlockSpec((toks, routes), lambda i: (0, 0)),
+        ],
+        out_shape=[
+            jax.ShapeDtypeStruct((toks, width), BF16),
+            jax.ShapeDtypeStruct((toks, routes), BF16),
+        ],
+        scratch_shapes=[pltpu.VMEM((toks, width), F32), pltpu.VMEM((toks, EXTRA), F32)],
         compiler_params=pltpu.CompilerParams(vmem_limit_bytes=VMEM_LIMIT),
         cost_estimate=pl.CostEstimate(
             flops=2 * total * toks * width * 2, bytes_accessed=total * wide * 2, transcendentals=0
@@ -273,25 +318,6 @@
 
 def exchange(x):
     return lax.all_to_all(x, AXES, split_axis=0, concat_axis=0, tiled=True)
-
-
-def gather_all(x):
-    return lax.all_gather(x, AXES, axis=0, tiled=False)
-
-
-def sort_pairs(x, experts):
-    x = x.reshape(experts * 8 // CHUNK, CHUNK // 8, 12)
-    first = x[:, :, :8].reshape(x.shape[0], -1)
-    last = x[:, :, 8:].reshape(x.shape[0], -1)
-    return jnp.concatenate([first, last], axis=1).reshape(-1)
-
-
-def unsort_pairs(x, experts):
-    chunks = experts * 8 // CHUNK
-    x = x.reshape(chunks, -1)
-    first = x[:, :CHUNK].reshape(chunks, CHUNK // 8, 8)
-    last = x[:, CHUNK:].reshape(chunks, CHUNK // 8, 4)
-    return jnp.concatenate([first, last], axis=2).reshape(-1)
 
 
 def body(
@@ -307,34 +333,20 @@
     saved_up,
 ):
     experts = lax.axis_size("group") * lax.axis_size("member")
-    me = lax.axis_index("group") * lax.axis_size("member") + lax.axis_index("member")
-    toks, width = tokens.shape
-    route_count = expert_ids.shape[1]
+    width = tokens.shape[1]
     pair_rows = saved_gate.shape[1] // experts
     packed_rows = experts * 8
     dest = expert_ids * pair_rows + pair_slot
     dest_t = expert_ids.T * pair_rows + pair_slot.T
 
-    sent_grads = pack(dest_t, grad_out, packed_rows)
-    here_grads = exchange(sent_grads)
-    here_tokens = exchange(pack(dest_t, tokens, packed_rows))
-
-    all_dest = gather_all(dest_t).reshape(experts, 1, -1)
-    all_gates = gather_all(gate_weights.T).reshape(experts, 1, -1)
-    wanted = (me * pair_rows + jnp.arange(pair_rows, dtype=jnp.int32))[None, :, None]
-    gates = jnp.sum(jnp.where(all_dest == wanted, all_gates.astype(F32), 0.0), axis=2)
-    gates = sort_pairs(gates, experts)[:, None]
+    gates_t = gate_weights.T.astype(F32)
+    here_grads = exchange(pack(dest_t, gates_t, grad_out, packed_rows, EXTRA))
+    here_tokens = exchange(pack(dest_t, gates_t, tokens, packed_rows, 0))
     a, b = sort_rows(saved_gate[0], saved_up[0])
-
-    back, grad_rows, hidden, pregate, preup, slot_gate = expert(
-        here_grads, gates, a, b, weight_gate[0], weight_up[0], weight_down[0]
+    back, grad_rows, hidden, pregate, preup = expert(
+        here_grads, a, b, weight_gate[0], weight_up[0], weight_down[0]
     )
     back_packed = exchange(back)
-
-    slot_gate = unsort_pairs(slot_gate.astype(BF16)[:, 0], experts)
-    all_slot_gates = gather_all(slot_gate)
-    mine = lax.dynamic_slice(all_slot_gates, (0, me * pair_rows), (experts, pair_rows))
-    grad_gates = jnp.take(mine.reshape(-1), dest.reshape(-1), axis=0, mode="clip")
 
     token_rows = unpack(here_tokens)
     over_rows = (((0,), (0,)), ((), ()))
@@ -342,10 +354,10 @@
     gate_total = lax.dot_general(token_rows, pregate, over_rows, preferred_element_type=F32)
     up_total = lax.dot_general(token_rows, preup, over_rows, preferred_element_type=F32)
 
-    grad_tokens = combine(dest, back_packed, toks)
+    grad_tokens, grad_gates = combine(dest, back_packed, width)
     return (
         grad_tokens,
-        grad_gates.reshape(toks, route_count),
+        grad_gates,
         gate_total[None].astype(BF16),
         up_total[None].astype(BF16),
         down_total[None].astype(BF16),

time: 433 us -> 284 us (0.66)
  blocking collectives: 240 us -> 0 us
  waiting for transfers between devices: 71 us -> 166 us
  local copies, waits for them, and re-layouts: 10.4 us -> 2.15 us
    all_gather x3 -> x0, blocking collectives: 240 us -> none  [gather_all(): return lax.all_gather(x, AXES, axis=0, tiled=False)]
    all_to_all x3, waiting for transfers between devices: 71 us -> 166 us  [exchange(): return lax.all_to_all(x, AXES, split_axis=0, concat_axis=0, tiled=True)]
    gather x1 -> x0, local copies, waits for them, and re-layouts: 6.8 us -> none  [body(): jnp.take(mine.reshape(-1), dest.reshape(-1), axis=0, mode='clip')]
  transfers between devices with their start and end apart: 3 -> 3, of which waited for: 1 -> 3; matrix products, arithmetic and copies ran while one was open for 8% -> 8% of each run, Pallas kernels for 11% -> 17%
where the time goes in v1:
time: 284 us; the launch traced here: 283 us
  waiting for transfers between devices  166 us (58%)
  Pallas kernels  60 us (21%)
  starting transfers between devices  29.3 us (10%)
  matrix products  22.7 us (8%)
    all_to_all x3, waiting for transfers between devices, exchange(): return lax.all_to_all(x, AXES, split_axis=0, concat_axis=0, tiled=True)  166 us
    all_to_all x3, starting transfers between devices, exchange(): return lax.all_to_all(x, AXES, split_axis=0, concat_axis=0, tiled=True)  29.3 us
    pallas_call x1, Pallas kernels, expert(): pl.pallas_call(expert_kernel, grid=(total // CHUNK,), in_specs=[packed_sp...  29 us
    pallas_call x2, Pallas kernels, pack(): pl.pallas_call(pack_kernel, grid=(packed_rows // CHUNK,), in_specs=[pl.Bl...  11.7 us
    dot_general x1, matrix products, body(): lax.dot_general(token_rows, pregate, over_rows, preferred_element_type=F32)  9.71 us
    pallas_call x1, Pallas kernels, combine(): pl.pallas_call(combine_kernel, grid=(total // CHUNK,), in_specs=[pl.Block...  6.83 us
    dot_general x1, matrix products, body(): lax.dot_general(token_rows, preup, over_rows, preferred_element_type=F32)  6.53 us
    dot_general x1, matrix products, body(): lax.dot_general(hidden, grad_rows, over_rows, preferred_element_type=F32)  6.47 us
  transfers between devices with their start and end apart: 3, of which 3 were waited for; matrix products, arithmetic and copies ran while one was open for 8% of the time, Pallas kernels for 17%

profile of v1, /device:TPU:1, one launch (start us, length us, event | category | flops | bytes accessed | tf_op | source)
XLA Modules:
  0.0 283.1 jit_solution(3712509263355796200)
XLA Ops:
  0.6 1.3 convert_bitcast_fusion.gate_ref
  1.9 1.3 multiply_add_fusion
  3.2 5.9 %shard_map.137 = bf16[1024,3200]{1,0:T(8,128)(2,1)} custom-call(s32[8,128]{1,0:T(8,128)} %bitcast.29, f32[8,128]{1,0:T(8,128)} %convert_bitcast_fusion.gate_ref, bf16[128,2048]{1,0:T(8,128)(2,1)} %x_ref.2), custom_call_target="tpu_custom_call" | custom-call | flops 1073741824 | bytes 6291456 | tf_op jit(solution)/shard_map/pallas_call | solution.py:68
  9.1 11.9 %all-to-all-start = ((bf16[128,8,3200]{2,1,0:T(8,128)(2,1)}), bf16[128,8,3200]{2,1,0:T(8,128)(2,1)}, u32[]{:S(2)}, u32[]{:S(2)}) async-start(bf16[128,8,3200]{2,1,0:T(8,128)(2,1)} %bitcast.26), calls=%async_computation | async-start | bytes 13107200 | tf_op jit(solution)/shard_map/all_to_all | solution.py:320
  21.0 5.8 %shard_map.141 = bf16[1024,3072]{1,0:T(8,128)(2,1)} custom-call(s32[8,128]{1,0:T(8,128)} %bitcast.30, f32[8,128]{1,0:T(8,128)} %convert_bitcast_fusion.gate_ref, bf16[128,2048]{1,0:T(8,128)(2,1)} %x_ref.3), custom_call_target="tpu_custom_call" | custom-call | flops 1073741824 | bytes 6291456 | tf_op jit(solution)/shard_map/pallas_call | solution.py:68
  26.9 73.9 %all-to-all-done = bf16[128,8,3200]{2,1,0:T(8,128)(2,1)} async-done(((bf16[128,8,3200]{2,1,0:T(8,128)(2,1)}), bf16[128,8,3200]{2,1,0:T(8,128)(2,1)}, u32[]{:S(2)}, u32[]{:S(2)}) %all-to-all-start) | async-done | bytes 6553632 | tf_op jit(solution)/shard_map/all_to_all | solution.py:320
  100.8 8.8 %all-to-all-start.2 = ((bf16[128,8,3072]{2,1,0:T(8,128)(2,1)}), bf16[128,8,3072]{2,1,0:T(8,128)(2,1)}, u32[]{:S(2)}, u32[]{:S(2)}) async-start(bf16[128,8,3072]{2,1,0:T(8,128)(2,1)} %bitcast.27), calls=%async_computation.2 | async-start | bytes 12582912 | tf_op jit(solution)/shard_map/all_to_all | solution.py:320
  109.6 6.0 %shard_map.138 = (bf16[1536,768]{1,0:T(8,128)(2,1)}, bf16[1536,768]{1,0:T(8,128)(2,1)}) custom-call(bf16[1536,768]{1,0:T(8,128)(2,1)} %bitcast.34, bf16[1536,768]{1,0:T(8,128)(2,1)} %bitcast.35), custom_call_target="tpu_custom_call" | custom-call | flops 1811939328 | bytes 9437184 | tf_op jit(solution)/shard_map/pallas_call | solution.py:103
  115.6 29.0 %shard_map.139 = (bf16[1024,3200]{1,0:T(8,128)(2,1)}, bf16[1536,2048]{1,0:T(8,128)(2,1)}, bf16[1536,768]{1,0:T(8,128)(2,1)}, bf16[1536,768]{1,0:T(8,128)(2,1)}, bf16[1536,768]{1,0:T(8,128)(2,1)}) custom-call(bf16[1024,3200]{1,0:T(8,128)(2,1)} %bitcast.3.packed_ref, bf16[1536,768]{1,0:T(8,128)(2,1)} %get-tuple-element.14.a_ref, ...), custom_call_target="tpu_custom_call" | custom-call | flops 14495514624 | bytes 19660800 | tf_op jit(solution)/shard_map/pallas_call | solution.py:212
  144.6 41.9 %all-to-all-done.2 = bf16[128,8,3072]{2,1,0:T(8,128)(2,1)} async-done(((bf16[128,8,3072]{2,1,0:T(8,128)(2,1)}), bf16[128,8,3072]{2,1,0:T(8,128)(2,1)}, u32[]{:S(2)}, u32[]{:S(2)}) %all-to-all-start.2) | async-done | bytes 6291488 | tf_op jit(solution)/shard_map/all_to_all | solution.py:320
  186.4 8.6 %all-to-all-start.1 = ((bf16[128,8,3200]{2,1,0:T(8,128)(2,1)}), bf16[128,8,3200]{2,1,0:T(8,128)(2,1)}, u32[]{:S(2)}, u32[]{:S(2)}) async-start(bf16[128,8,3200]{2,1,0:T(8,128)(2,1)} %bitcast.28), calls=%async_computation.1 | async-start | bytes 13107200 | tf_op jit(solution)/shard_map/all_to_all | solution.py:320
  195.1 0.0 copy-done.1
  195.1 0.7 copy.15.dest_ref
  195.8 6.5 %shard_map.142 = bf16[1536,2048]{1,0:T(8,128)(2,1)} custom-call(bf16[1024,3072]{1,0:T(8,128)(2,1)} %bitcast.12.packed_ref), custom_call_target="tpu_custom_call" | custom-call | flops 1073741824 | bytes 12582912 | tf_op jit(solution)/shard_map/pallas_call | solution.py:137
  202.2 0.0 copy-done.4
  202.3 0.0 slice-start
  202.3 9.7 %fusion = bf16[1,2048,768]{2,1,0:T(8,128)(2,1)} fusion(bf16[1536,2048]{1,0:T(8,128)(2,1)} %shard_map.142, bf16[1536,768]{1,0:T(8,128)(2,1)S(1)} %copy-done.4), kind=kOutput, calls=%fused_computation.3 | convolution fusion | flops 4833411072 | bytes 11796480 | tf_op jit(solution)/shard_map/dot_general | solution.py:354
  212.0 0.0 copy-done
  212.0 6.5 %fusion.1 = bf16[1,2048,768]{2,1,0:T(8,128)(2,1)} fusion(bf16[1536,2048]{1,0:T(8,128)(2,1)S(1)} %copy-done, bf16[1536,768]{1,0:T(8,128)(2,1)S(1)} %copy-done.3), kind=kOutput, calls=%fused_computation.4 | convolution fusion | flops 4833411072 | bytes 11796480 | tf_op jit(solution)/shard_map/dot_general | solution.py:355
  218.5 0.0 slice-done.1
  218.5 6.5 %fusion.2 = bf16[1,768,2048]{2,1,0:T(8,128)(2,1)} fusion(bf16[1536,768]{1,0:T(8,128)(2,1)S(1)} %copy-done.2, bf16[1536,2048]{1,0:T(8,128)(2,1)S(1)} %bitcast.37), kind=kOutput, calls=%fused_computation.5 | convolution fusion | flops 4833411072 | bytes 11796480 | tf_op jit(solution)/shard_map/dot_general | solution.py:353
  225.0 49.8 %all-to-all-done.1 = bf16[128,8,3200]{2,1,0:T(8,128)(2,1)} async-done(((bf16[128,8,3200]{2,1,0:T(8,128)(2,1)}), bf16[128,8,3200]{2,1,0:T(8,128)(2,1)}, u32[]{:S(2)}, u32[]{:S(2)}) %all-to-all-start.1) | async-done | bytes 6553632 | tf_op jit(solution)/shard_map/all_to_all | solution.py:320
  274.8 6.8 %shard_map.140 = (bf16[128,2048]{1,0:T(8,128)(2,1)}, bf16[128,8]{1,0:T(8,128)(2,1)}) custom-call(s32[128,8]{1,0:T(8,128)} %copy.15.dest_ref, bf16[1024,3200]{1,0:T(8,128)(2,1)} %bitcast.10.packed_ref), custom_call_target="tpu_custom_call" | custom-call | flops 1073741824 | bytes 6553600 | tf_op jit(solution)/shard_map/pallas_call | solution.py:296
  281.7 1.4 copy.16
  (10 shorter events, 0.0 us)
Async XLA Ops:
  9.1 91.7 %all-to-all-start = ((bf16[128,8,3200]{2,1,0:T(8,128)(2,1)}), bf16[128,8,3200]{2,1,0:T(8,128)(2,1)}, u32[]{:S(2)}, u32[]{:S(2)}) async-start(bf16[128,8,3200]{2,1,0:T(8,128)(2,1)} %bitcast.26), calls=%async_computation | async-start | bytes 13107200 | tf_op jit(solution)/shard_map/all_to_all | solution.py:320
  100.8 85.6 %all-to-all-start.2 = ((bf16[128,8,3072]{2,1,0:T(8,128)(2,1)}), bf16[128,8,3072]{2,1,0:T(8,128)(2,1)}, u32[]{:S(2)}, u32[]{:S(2)}) async-start(bf16[128,8,3072]{2,1,0:T(8,128)(2,1)} %bitcast.27), calls=%async_computation.2 | async-start | bytes 12582912 | tf_op jit(solution)/shard_map/all_to_all | solution.py:320
  186.4 8.6 %copy-start.1 = (s32[128,8]{0,1:T(8,128)S(1)}, s32[128,8]{0,1:T(8,128)}, u32[]{:S(2)}) copy-start(s32[128,8]{0,1:T(8,128)} %multiply_add_fusion) | copy-start | bytes 12292
  186.4 88.4 %all-to-all-start.1 = ((bf16[128,8,3200]{2,1,0:T(8,128)(2,1)}), bf16[128,8,3200]{2,1,0:T(8,128)(2,1)}, u32[]{:S(2)}, u32[]{:S(2)}) async-start(bf16[128,8,3200]{2,1,0:T(8,128)(2,1)} %bitcast.28), calls=%async_computation.1 | async-start | bytes 13107200 | tf_op jit(solution)/shard_map/all_to_all | solution.py:320
  195.8 6.5 %copy-start.4 = (bf16[1536,768]{1,0:T(8,128)(2,1)S(1)}, bf16[1536,768]{1,0:T(8,128)(2,1)}, u32[]{:S(2)}) copy-start(bf16[1536,768]{1,0:T(8,128)(2,1)} %get-tuple-element.19) | copy-start | bytes 7077892
  202.2 9.7 %copy-start = (bf16[1536,2048]{1,0:T(8,128)(2,1)S(1)}, bf16[1536,2048]{1,0:T(8,128)(2,1)}, u32[]{:S(2)}) copy-start(bf16[1536,2048]{1,0:T(8,128)(2,1)} %shard_map.142) | copy-start | bytes 18874372
  202.3 9.7 %copy-start.3 = (bf16[1536,768]{1,0:T(8,128)(2,1)S(1)}, bf16[1536,768]{1,0:T(8,128)(2,1)}, u32[]{:S(2)}) copy-start(bf16[1536,768]{1,0:T(8,128)(2,1)} %get-tuple-element.20) | copy-start | bytes 7077892
  202.3 16.3 %slice-start = ((s8[6291456]{0:T(1024)(128)(4,1)}), s8[4194304]{0:T(1024)(128)(4,1)S(1)}, s32[]{:S(2)}) async-start(s8[6291456]{0:T(1024)(128)(4,1)} %bitcast.36), calls=%async_computation.3 | async-start | bytes 8388608
  212.0 6.5 %slice-start.1 = ((s8[6291456]{0:T(1024)(128)(4,1)}), s8[2097152]{0:T(1024)(128)(4,1)S(1)}, s32[]{:S(2)}) async-start(s8[6291456]{0:T(1024)(128)(4,1)} %bitcast.36), calls=%async_computation.4 | async-start | bytes 4194304
  212.0 6.5 %copy-start.2 = (bf16[1536,768]{1,0:T(8,128)(2,1)S(1)}, bf16[1536,768]{1,0:T(8,128)(2,1)}, u32[]{:S(2)}) copy-start(bf16[1536,768]{1,0:T(8,128)(2,1)} %get-tuple-element.21) | copy-start | bytes 7077892

commit v2 on v1

--- a/solution.py
+++ b/solution.py
@@ -33,43 +33,44 @@
     return jnp.where(lane < EXTRA // 2, a, b).astype(BF16)
 
 
-def pack_kernel(dest_ref, gate_ref, x_ref, out_ref):
+def pack_kernel(ids_ref, slot_ref, gate_ref, x_ref, out_ref):
+    dest = ids_ref[...] * 12 + slot_ref[...]
     rows, toks = out_ref.shape[0], x_ref.shape[0]
     width = x_ref.shape[1]
     half = width // 2
     index = lax.broadcasted_iota(jnp.int32, (rows, toks), 0) + pl.program_id(0) * rows
     id_a, id_b, first = packed_ids(index)
-    hit_a = dest_ref[0:1, :] == id_a
-    hit_b = dest_ref[0:1, :] == id_b
-    for k in range(1, dest_ref.shape[0]):
-        d = dest_ref[k : k + 1, :]
-        hit_a = hit_a | (d == id_a)
-        hit_b = hit_b | (d == id_b)
+    gate = gate_ref[...].astype(F32)
+    hit_a = index < 0
+    hit_b = index < 0
+    gate_a = jnp.zeros((rows, toks), F32)
+    gate_b = jnp.zeros((rows, toks), F32)
+    for k in range(dest.shape[0]):
+        d, g = dest[k : k + 1, :], gate[k : k + 1, :]
+        here_a = d == id_a
+        here_b = d == id_b
+        hit_a = hit_a | here_a
+        hit_b = hit_b | here_b
+        gate_a = jnp.where(here_a, g, gate_a)
+        gate_b = jnp.where(here_b, g, gate_b)
     out_ref[:, :width] = dot(zero_one(hit_a), x_ref[...]).astype(BF16)
     low = dot(zero_one(hit_b & first), x_ref[:, :half])
     high = dot(zero_one(hit_b & jnp.logical_not(first)), x_ref[:, half:])
     out_ref[:, width : width + half] = (low + high).astype(BF16)
-    if out_ref.shape[1] > width + half:
-        gate_a = jnp.zeros((rows, toks), F32)
-        gate_b = jnp.zeros((rows, toks), F32)
-        for k in range(dest_ref.shape[0]):
-            d = dest_ref[k : k + 1, :]
-            g = gate_ref[k : k + 1, :]
-            gate_a = jnp.where(d == id_a, g, gate_a)
-            gate_b = jnp.where(d == id_b, g, gate_b)
-        out_ref[:, width + half :] = side_by_side(
-            jnp.sum(gate_a, axis=1, keepdims=True), jnp.sum(gate_b, axis=1, keepdims=True)
-        )
-
-
-def pack(dest_t, gates_t, x, packed_rows, extra):
+    out_ref[:, width + half :] = side_by_side(
+        jnp.sum(gate_a, axis=1, keepdims=True), jnp.sum(gate_b, axis=1, keepdims=True)
+    )
+
+
+def pack(ids_t, slot_t, gates_t, x, packed_rows):
     toks, width = x.shape
-    wide = width * 3 // 2 + extra
+    wide = width * 3 // 2 + EXTRA
     return pl.pallas_call(
         pack_kernel,
         grid=(packed_rows // CHUNK,),
         in_specs=[
-            pl.BlockSpec(dest_t.shape, lambda i: (0, 0)),
+            pl.BlockSpec(ids_t.shape, lambda i: (0, 0)),
+            pl.BlockSpec(slot_t.shape, lambda i: (0, 0)),
             pl.BlockSpec(gates_t.shape, lambda i: (0, 0)),
             pl.BlockSpec(x.shape, lambda i: (0, 0)),
         ],
@@ -81,7 +82,7 @@
             bytes_accessed=packed_rows * width * 3,
             transcendentals=0,
         ),
-    )(dest_t, gates_t, x)
+    )(ids_t, slot_t, gates_t, x)
 
 
 def sort_kernel(a_ref, b_ref, out_a, out_b):
@@ -131,20 +132,74 @@
     rows_ref[packed:, half:] = dot(high, rest).astype(BF16)
 
 
-def unpack(packed):
-    total, wide = packed.shape
-    width = wide * 2 // 3
-    return pl.pallas_call(
-        unpack_into,
-        grid=(total // CHUNK,),
-        in_specs=[pl.BlockSpec((CHUNK, wide), lambda i: (i, 0))],
-        out_specs=pl.BlockSpec((CHUNK * 3 // 2, width), lambda i: (i, 0)),
-        out_shape=jax.ShapeDtypeStruct((total * 3 // 2, width), BF16),
-        compiler_params=pltpu.CompilerParams(vmem_limit_bytes=VMEM_LIMIT),
-        cost_estimate=pl.CostEstimate(
-            flops=total * CHUNK * width * 2, bytes_accessed=total * wide * 4, transcendentals=0
-        ),
-    )(packed)
+def spread_kernel(x_ref, out_ref):
+    groups, rows, width = out_ref.shape
+    toks = x_ref.shape[0]
+    me = lax.axis_index("member")
+    extra = x_ref[:, width:]
+    lane = lax.broadcasted_iota(jnp.int32, (16, EXTRA), 1)
+    pick = zero_one(lane == lax.broadcasted_iota(jnp.int32, (16, EXTRA), 0))
+    table = lax.dot_general(pick, extra, NT, preferred_element_type=F32).astype(jnp.int32)
+    ids, slots = table[:8, :], table[8:, :]
+    source = lax.broadcasted_iota(jnp.int32, (8, toks), 1) >> 7
+    keys = jnp.where((ids & 7) == me, (ids >> 3) * 12 + slots + source * 256, -1)
+    index = lax.broadcasted_iota(jnp.int32, (groups * rows, 1), 0)
+    group = (index * 1366) >> 16
+    row = index - group * rows
+    early = row < rows * 2 // 3
+    late = row - rows * 2 // 3
+    wanted = group * 12 + jnp.where(
+        early, (row & 7) + (row >> 3) * 256, 8 + (late & 3) + (late >> 2) * 256
+    )
+    hit = keys[0:1, :] == wanted
+    for k in range(1, 8):
+        hit = hit | (keys[k : k + 1, :] == wanted)
+    moved = dot(zero_one(hit), x_ref[:, :width]).astype(BF16)
+    out_ref[...] = moved.reshape(out_ref.shape)
+
+
+def spread(x, groups, width):
+    total, wide = x.shape
+    step = total // 2
+    return pl.pallas_call(
+        spread_kernel,
+        grid=(2,),
+        in_specs=[pl.BlockSpec((step, wide), lambda i: (i, 0))],
+        out_specs=pl.BlockSpec((groups, 48, width), lambda i: (0, i, 0)),
+        out_shape=jax.ShapeDtypeStruct((groups, 96, width), BF16),
+        compiler_params=pltpu.CompilerParams(vmem_limit_bytes=VMEM_LIMIT),
+        cost_estimate=pl.CostEstimate(
+            flops=2 * groups * 96 * step * width,
+            bytes_accessed=2 * (total * wide + groups * 96 * width),
+            transcendentals=0,
+        ),
+    )(x)
+
+
+def collect_kernel(x_ref, out_ref):
+    late = out_ref.shape[0] * 2 // 3
+    for group in range(x_ref.shape[0]):
+        for part in range(2):
+            at = part * 48
+            to = (group * 2 + part) * 32
+            out_ref[to : to + 32, :] = x_ref[group, at : at + 32, :]
+            to = late + (group * 2 + part) * 16
+            out_ref[to : to + 16, :] = x_ref[group, at + 32 : at + 48, :]
+
+
+def collect(x):
+    groups, rows, width = x.shape
+    return pl.pallas_call(
+        collect_kernel,
+        grid=(groups // 4,),
+        in_specs=[pl.BlockSpec((4, rows, width), lambda i: (i, 0, 0))],
+        out_specs=pl.BlockSpec((4 * rows, width), lambda i: (i, 0)),
+        out_shape=jax.ShapeDtypeStruct((groups * rows, width), BF16),
+        compiler_params=pltpu.CompilerParams(vmem_limit_bytes=VMEM_LIMIT),
+        cost_estimate=pl.CostEstimate(
+            flops=0, bytes_accessed=groups * rows * width * 4, transcendentals=0
+        ),
+    )(x)
 
 
 def expert_kernel(
@@ -287,7 +342,11 @@
     @pl.when(step == pl.num_programs(0) - 1)
     def _():
         out_ref[...] = acc_ref[...].astype(BF16)
-        gate_ref[...] = gates[:, : gate_ref.shape[1]].astype(BF16)
+        row = lax.broadcasted_iota(jnp.int32, (16, EXTRA), 0)
+        turned = lax.dot_general(
+            zero_one(lane == row), gates.astype(BF16), NT, preferred_element_type=F32
+        )
+        gate_ref[...] = turned[: gate_ref.shape[0], :].astype(BF16)
 
 
 def combine(dest, packed, width):
@@ -302,11 +361,11 @@
         ],
         out_specs=[
             pl.BlockSpec((toks, width), lambda i: (0, 0)),
-            pl.BlockSpec((toks, routes), lambda i: (0, 0)),
+            pl.BlockSpec((routes, toks), lambda i: (0, 0)),
         ],
         out_shape=[
             jax.ShapeDtypeStruct((toks, width), BF16),
-            jax.ShapeDtypeStruct((toks, routes), BF16),
+            jax.ShapeDtypeStruct((routes, toks), BF16),
         ],
         scratch_shapes=[pltpu.VMEM((toks, width), F32), pltpu.VMEM((toks, EXTRA), F32)],
         compiler_params=pltpu.CompilerParams(vmem_limit_bytes=VMEM_LIMIT),
@@ -316,8 +375,8 @@
     )(dest, packed)
 
 
-def exchange(x):
-    return lax.all_to_all(x, AXES, split_axis=0, concat_axis=0, tiled=True)
+def exchange(x, axes):
+    return lax.all_to_all(x, axes, split_axis=0, concat_axis=0, tiled=True)
 
 
 def body(
@@ -337,18 +396,25 @@
     pair_rows = saved_gate.shape[1] // experts
     packed_rows = experts * 8
     dest = expert_ids * pair_rows + pair_slot
-    dest_t = expert_ids.T * pair_rows + pair_slot.T
-
-    gates_t = gate_weights.T.astype(F32)
-    here_grads = exchange(pack(dest_t, gates_t, grad_out, packed_rows, EXTRA))
-    here_tokens = exchange(pack(dest_t, gates_t, tokens, packed_rows, 0))
+    sent_grads = pack(expert_ids.T, pair_slot.T, gate_weights.T, grad_out, packed_rows)
+    sent_grads, expert_ids, tokens = lax.optimization_barrier((sent_grads, expert_ids, tokens))
+    routes = jnp.concatenate([expert_ids, pair_slot], axis=1).astype(BF16)
+    routes = jnp.pad(routes, ((0, 0), (0, EXTRA - routes.shape[1])))
+    line_tokens = lax.all_gather(
+        jnp.concatenate([tokens, routes], axis=1), "member", axis=0, tiled=True
+    )
+    here_grads = exchange(sent_grads, AXES)
+    sent_tokens = spread(line_tokens, lax.axis_size("group"), width)
+    here_grads, sent_tokens = lax.optimization_barrier((here_grads, sent_tokens))
+    here_tokens = exchange(sent_tokens, "group")
     a, b = sort_rows(saved_gate[0], saved_up[0])
     back, grad_rows, hidden, pregate, preup = expert(
         here_grads, a, b, weight_gate[0], weight_up[0], weight_down[0]
     )
-    back_packed = exchange(back)
-
-    token_rows = unpack(here_tokens)
+    back, here_tokens = lax.optimization_barrier((back, here_tokens))
+    back_packed = exchange(back, AXES)
+
+    token_rows = collect(here_tokens)
     over_rows = (((0,), (0,)), ((), ()))
     down_total = lax.dot_general(hidden, grad_rows, over_rows, preferred_element_type=F32)
     gate_total = lax.dot_general(token_rows, pregate, over_rows, preferred_element_type=F32)
@@ -357,7 +423,7 @@
     grad_tokens, grad_gates = combine(dest, back_packed, width)
     return (
         grad_tokens,
-        grad_gates,
+        grad_gates.T,
         gate_total[None].astype(BF16),
         up_total[None].astype(BF16),
         down_total[None].astype(BF16),

time: 284 us -> 333 us (1.17)
  waiting for transfers between devices: 166 us -> 200 us
  between operations: 0.71 us -> 14.1 us
  Pallas kernels: 60 us -> 63.7 us
    all_gather x0 -> x1, waiting for transfers between devices: none -> 94.1 us  [body(): lax.all_gather(jnp.concatenate([tokens, routes], axis=1), 'member', axis=...]
    all_to_all x3, waiting for transfers between devices: 166 us -> 106 us  [exchange(): return lax.all_to_all(x, axes, split_axis=0, concat_axis=0, tiled=True)]
    pallas_call x1 -> x2, Pallas kernels: 6.45 us -> 15.4 us  [the longest x1 9.24 us: spread(): pl.pallas_call(spread_kernel, grid=(2,), in_specs=[pl.BlockSpec((step, wi...]
    pallas_call x2 -> x1, Pallas kernels: 11.7 us -> 6.34 us  [pack(): pl.pallas_call(pack_kernel, grid=(packed_rows // CHUNK,), in_specs=[pl.Bl...]
  transfers between devices with their start and end apart: 3 -> 4, of which waited for: 3 -> 3; matrix products, arithmetic and copies ran while one was open for 8% -> 8% of each run, Pallas kernels for 17% -> 15%
where the time goes in v2:
time: 333 us
  waiting for transfers between devices  200 us (60%)
  Pallas kernels  63.7 us (19%)
  starting transfers between devices  26.7 us (8%)
  matrix products  25.7 us (8%)
  between operations  14.1 us (4%)
    all_to_all x3, waiting for transfers between devices, exchange(): return lax.all_to_all(x, axes, split_axis=0, concat_axis=0, tiled=True)  106 us
    all_gather x1, waiting for transfers between devices, body(): lax.all_gather(jnp.concatenate([tokens, routes], axis=1), 'member', axis=...  94.1 us
    pallas_call x1, Pallas kernels, expert(): pl.pallas_call(expert_kernel, grid=(total // CHUNK,), in_specs=[packed_sp...  28.9 us
    all_to_all x3, starting transfers between devices, exchange(): return lax.all_to_all(x, axes, split_axis=0, concat_axis=0, tiled=True)  26.7 us
    dot_general x1, matrix products, body(): lax.dot_general(token_rows, preup, over_rows, preferred_element_type=F32)  9.72 us
    dot_general x1, matrix products, body(): lax.dot_general(hidden, grad_rows, over_rows, preferred_element_type=F32)  9.3 us
    pallas_call x1, Pallas kernels, spread(): pl.pallas_call(spread_kernel, grid=(2,), in_specs=[pl.BlockSpec((step, wi...  9.24 us
    pallas_call x1, Pallas kernels, combine(): pl.pallas_call(combine_kernel, grid=(total // CHUNK,), in_specs=[pl.Block...  6.95 us
  transfers between devices with their start and end apart: 4, of which 3 were waited for; matrix products, arithmetic and copies ran while one was open for 8% of the time, Pallas kernels for 15%

profile of v2, /device:TPU:1, one launch (start us, length us, event | category | flops | bytes accessed | tf_op | source)
XLA Modules:
  0.0 332.6 jit_solution(11821557713007604095)
XLA Ops:
  7.2 0.0 all-gather.2.cloned.1.call-start
  7.2 0.8 fusion.5
  8.0 6.3 %shard_map.137 = bf16[1024,3200]{1,0:T(8,128)(2,1)} custom-call(s32[8,128]{1,0:T(8,128)} %bitcast.27, s32[8,128]{1,0:T(8,128)} %bitcast.28, bf16[8,128]{1,0:T(8,128)(2,1)} %bitcast.29, bf16[128,2048]{1,0:T(8,128)(2,1)} %x_ref.1), custom_call_target="tpu_custom_call" | custom-call | flops 1073741824 | bytes 6291456 | tf_op jit(solution)/shard_map/pallas_call | solution.py:68
  14.3 0.0 copy-done.2
  14.3 0.1 copy.24
  14.5 0.9 fusion.4
  15.3 0.0 all-gather.2.cloned.1.call-update
  15.4 11.9 %all-to-all-start = ((bf16[128,8,3200]{2,1,0:T(8,128)(2,1)}), bf16[128,8,3200]{2,1,0:T(8,128)(2,1)}, u32[]{:S(2)}, u32[]{:S(2)}) async-start(bf16[128,8,3200]{2,1,0:T(8,128)(2,1)} %bitcast.25), calls=%async_computation | async-start | bytes 13107200 | tf_op jit(solution)/shard_map/all_to_all | solution.py:379
  27.3 94.1 %all-gather.2.cloned.1.call-done.x_ref = bf16[1024,2176]{1,0:T(8,128)(2,1)} async-done(((bf16[128,2176]{1,0:T(8,128)(2,1)}), bf16[1024,2176]{1,0:T(8,128)(2,1)}) %all-gather.2.cloned.1.call-update) | async-done | bytes 4456464 | tf_op jit(solution)/shard_map/all_gather | solution.py:403
  121.4 9.2 %shard_map.138 = bf16[16,96,2048]{2,1,0:T(8,128)(2,1)} custom-call(bf16[1024,2176]{1,0:T(8,128)(2,1)} %all-gather.2.cloned.1.call-done.x_ref), custom_call_target="tpu_custom_call" | custom-call | flops 3221225472 | bytes 10747904 | tf_op jit(solution)/shard_map/pallas_call | solution.py:164
  130.6 0.0 all-to-all-done
  130.6 6.8 %all-to-all-start.1 = ((bf16[16,96,2048]{2,1,0:T(8,128)(2,1)}), bf16[16,96,2048]{2,1,0:T(8,128)(2,1)}, u32[]{:S(2)}, u32[]{:S(2)}) async-start(bf16[16,96,2048]{2,1,0:T(8,128)(2,1)} %shard_map.138), calls=%async_computation.1 | async-start | bytes 12582912 | tf_op jit(solution)/shard_map/all_to_all | solution.py:379
  137.5 6.0 %shard_map.139 = (bf16[1536,768]{1,0:T(8,128)(2,1)}, bf16[1536,768]{1,0:T(8,128)(2,1)}) custom-call(bf16[1536,768]{1,0:T(8,128)(2,1)} %bitcast.33, bf16[1536,768]{1,0:T(8,128)(2,1)} %bitcast.34), custom_call_target="tpu_custom_call" | custom-call | flops 1811939328 | bytes 9437184 | tf_op jit(solution)/shard_map/pallas_call | solution.py:104
  143.5 28.9 %shard_map.140 = (bf16[1024,3200]{1,0:T(8,128)(2,1)}, bf16[1536,2048]{1,0:T(8,128)(2,1)}, bf16[1536,768]{1,0:T(8,128)(2,1)}, bf16[1536,768]{1,0:T(8,128)(2,1)}, bf16[1536,768]{1,0:T(8,128)(2,1)}) custom-call(bf16[1024,3200]{1,0:T(8,128)(2,1)} %bitcast.4.packed_ref, bf16[1536,768]{1,0:T(8,128)(2,1)} %get-tuple-element.25.a_ref, ...), custom_call_target="tpu_custom_call" | custom-call | flops 14495514624 | bytes 19660800 | tf_op jit(solution)/shard_map/pallas_call | solution.py:267
  172.4 58.7 %all-to-all-done.1.x_ref = bf16[16,96,2048]{2,1,0:T(8,128)(2,1)} async-done(((bf16[16,96,2048]{2,1,0:T(8,128)(2,1)}), bf16[16,96,2048]{2,1,0:T(8,128)(2,1)}, u32[]{:S(2)}, u32[]{:S(2)}) %all-to-all-start.1) | async-done | bytes 6291488 | tf_op jit(solution)/shard_map/all_to_all | solution.py:379
  231.1 7.9 %all-to-all-start.2 = ((bf16[128,8,3200]{2,1,0:T(8,128)(2,1)}), bf16[128,8,3200]{2,1,0:T(8,128)(2,1)}, u32[]{:S(2)}, u32[]{:S(2)}) async-start(bf16[128,8,3200]{2,1,0:T(8,128)(2,1)} %bitcast.26), calls=%async_computation.2 | async-start | bytes 13107200 | tf_op jit(solution)/shard_map/all_to_all | solution.py:379
  239.1 0.7 copy.25.dest_ref
  239.8 9.3 %fusion.2 = bf16[1,768,2048]{2,1,0:T(8,128)(2,1)} fusion(bf16[1536,768]{1,0:T(8,128)(2,1)S(1)} %copy-done.3, bf16[1536,2048]{1,0:T(8,128)(2,1)} %get-tuple-element.36), kind=kOutput, calls=%fused_computation.5 | convolution fusion | flops 4833411072 | bytes 11796480 | tf_op jit(solution)/shard_map/dot_general | solution.py:419
  249.1 6.2 %shard_map.142 = bf16[1536,2048]{1,0:T(8,128)(2,1)} custom-call(bf16[16,96,2048]{2,1,0:T(8,128)(2,1)} %all-to-all-done.1.x_ref), custom_call_target="tpu_custom_call" | custom-call | bytes 12582912 | tf_op jit(solution)/shard_map/pallas_call | solution.py:192
  255.3 9.7 %fusion.1 = bf16[1,2048,768]{2,1,0:T(8,128)(2,1)} fusion(bf16[1536,2048]{1,0:T(8,128)(2,1)} %shard_map.142, bf16[1536,768]{1,0:T(8,128)(2,1)S(1)} %copy-done.5), kind=kOutput, calls=%fused_computation.4 | convolution fusion | flops 4833411072 | bytes 11796480 | tf_op jit(solution)/shard_map/dot_general | solution.py:421
  265.0 0.0 copy-done
  265.0 6.7 %fusion = bf16[1,2048,768]{2,1,0:T(8,128)(2,1)} fusion(bf16[1536,2048]{1,0:T(8,128)(2,1)S(1)} %copy-done, bf16[1536,768]{1,0:T(8,128)(2,1)S(1)} %copy-done.4), kind=kOutput, calls=%fused_computation.3 | convolution fusion | flops 4833411072 | bytes 11796480 | tf_op jit(solution)/shard_map/dot_general | solution.py:420
  271.7 47.1 %all-to-all-done.2 = bf16[128,8,3200]{2,1,0:T(8,128)(2,1)} async-done(((bf16[128,8,3200]{2,1,0:T(8,128)(2,1)}), bf16[128,8,3200]{2,1,0:T(8,128)(2,1)}, u32[]{:S(2)}, u32[]{:S(2)}) %all-to-all-start.2) | async-done | bytes 6553632 | tf_op jit(solution)/shard_map/all_to_all | solution.py:379
  318.8 7.0 %shard_map.141 = (bf16[128,2048]{1,0:T(8,128)(2,1)}, bf16[8,128]{1,0:T(8,128)(2,1)}) custom-call(s32[128,8]{1,0:T(8,128)} %copy.25.dest_ref, bf16[1024,3200]{1,0:T(8,128)(2,1)} %bitcast.11.packed_ref), custom_call_target="tpu_custom_call" | custom-call | flops 1073741824 | bytes 6553600 | tf_op jit(solution)/shard_map/pallas_call | solution.py:355
  (12 shorter events, 0.0 us)
Async XLA Ops:
  7.2 114.2 %all-gather.2.cloned.1.call-start = ((), (), s32[]{:S(2)}) async-start(), calls=%async_computation.3 | async-start | bytes 5013504 | tf_op jit(solution)/shard_map/all_gather | solution.py:403
  8.0 6.4 %copy-start.2 = (s32[128,8]{0,1:T(8,128)S(1)}, s32[128,8]{0,1:T(8,128)}, u32[]{:S(2)}) copy-start(s32[128,8]{0,1:T(8,128)} %param.12) | copy-start | bytes 12292
  8.0 6.5 %copy-start.1 = (bf16[128,2048]{1,0:T(8,128)(2,1)S(1)}, bf16[128,2048]{1,0:T(8,128)(2,1)}, u32[]{:S(2)}) copy-start(bf16[128,2048]{1,0:T(8,128)(2,1)} %param.10) | copy-start | bytes 1572868
  15.4 115.3 %all-to-all-start = ((bf16[128,8,3200]{2,1,0:T(8,128)(2,1)}), bf16[128,8,3200]{2,1,0:T(8,128)(2,1)}, u32[]{:S(2)}, u32[]{:S(2)}) async-start(bf16[128,8,3200]{2,1,0:T(8,128)(2,1)} %bitcast.25), calls=%async_computation | async-start | bytes 13107200 | tf_op jit(solution)/shard_map/all_to_all | solution.py:379
  130.6 100.5 %all-to-all-start.1 = ((bf16[16,96,2048]{2,1,0:T(8,128)(2,1)}), bf16[16,96,2048]{2,1,0:T(8,128)(2,1)}, u32[]{:S(2)}, u32[]{:S(2)}) async-start(bf16[16,96,2048]{2,1,0:T(8,128)(2,1)} %shard_map.138), calls=%async_computation.1 | async-start | bytes 12582912 | tf_op jit(solution)/shard_map/all_to_all | solution.py:379
  231.1 8.7 %copy-start.3 = (bf16[1536,768]{1,0:T(8,128)(2,1)S(1)}, bf16[1536,768]{1,0:T(8,128)(2,1)}, u32[]{:S(2)}) copy-start(bf16[1536,768]{1,0:T(8,128)(2,1)} %get-tuple-element.35) | copy-start | bytes 7077892
  231.1 87.7 %all-to-all-start.2 = ((bf16[128,8,3200]{2,1,0:T(8,128)(2,1)}), bf16[128,8,3200]{2,1,0:T(8,128)(2,1)}, u32[]{:S(2)}, u32[]{:S(2)}) async-start(bf16[128,8,3200]{2,1,0:T(8,128)(2,1)} %bitcast.26), calls=%async_computation.2 | async-start | bytes 13107200 | tf_op jit(solution)/shard_map/all_to_all | solution.py:379
  249.1 6.2 %copy-start.5 = (bf16[1536,768]{1,0:T(8,128)(2,1)S(1)}, bf16[1536,768]{1,0:T(8,128)(2,1)}, u32[]{:S(2)}) copy-start(bf16[1536,768]{1,0:T(8,128)(2,1)} %get-tuple-element.34) | copy-start | bytes 7077892
  255.3 9.7 %copy-start = (bf16[1536,2048]{1,0:T(8,128)(2,1)S(1)}, bf16[1536,2048]{1,0:T(8,128)(2,1)}, u32[]{:S(2)}) copy-start(bf16[1536,2048]{1,0:T(8,128)(2,1)} %shard_map.142) | copy-start | bytes 18874372
  255.3 9.7 %copy-start.4 = (bf16[1536,768]{1,0:T(8,128)(2,1)S(1)}, bf16[1536,768]{1,0:T(8,128)(2,1)}, u32[]{:S(2)}) copy-start(bf16[1536,768]{1,0:T(8,128)(2,1)} %get-tuple-element.33) | copy-start | bytes 7077892
Sparse Core Ops, SparseCore 0:
  15.5 105.8 all-gather.1

commit v3 on v1

--- a/solution.py
+++ b/solution.py
@@ -1,3 +1,5 @@
+import functools
+
 import jax
 import jax.numpy as jnp
 from jax import lax
@@ -33,55 +35,56 @@
     return jnp.where(lane < EXTRA // 2, a, b).astype(BF16)
 
 
-def pack_kernel(dest_ref, gate_ref, x_ref, out_ref):
+def pack_kernel(scaled, ids_ref, slot_ref, gate_ref, x_ref, out_ref, halves_ref):
     rows, toks = out_ref.shape[0], x_ref.shape[0]
     width = x_ref.shape[1]
     half = width // 2
+
+    @pl.when(pl.program_id(0) == 0)
+    def _():
+        halves_ref[:toks, :] = x_ref[:, :half]
+        halves_ref[toks:, :] = x_ref[:, half:]
+
     index = lax.broadcasted_iota(jnp.int32, (rows, toks), 0) + pl.program_id(0) * rows
     id_a, id_b, first = packed_ids(index)
-    hit_a = dest_ref[0:1, :] == id_a
-    hit_b = dest_ref[0:1, :] == id_b
-    for k in range(1, dest_ref.shape[0]):
-        d = dest_ref[k : k + 1, :]
-        hit_a = hit_a | (d == id_a)
-        hit_b = hit_b | (d == id_b)
-    out_ref[:, :width] = dot(zero_one(hit_a), x_ref[...]).astype(BF16)
-    low = dot(zero_one(hit_b & first), x_ref[:, :half])
-    high = dot(zero_one(hit_b & jnp.logical_not(first)), x_ref[:, half:])
-    out_ref[:, width : width + half] = (low + high).astype(BF16)
-    if out_ref.shape[1] > width + half:
-        gate_a = jnp.zeros((rows, toks), F32)
-        gate_b = jnp.zeros((rows, toks), F32)
-        for k in range(dest_ref.shape[0]):
-            d = dest_ref[k : k + 1, :]
-            g = gate_ref[k : k + 1, :]
-            gate_a = jnp.where(d == id_a, g, gate_a)
-            gate_b = jnp.where(d == id_b, g, gate_b)
-        out_ref[:, width + half :] = side_by_side(
-            jnp.sum(gate_a, axis=1, keepdims=True), jnp.sum(gate_b, axis=1, keepdims=True)
-        )
-
-
-def pack(dest_t, gates_t, x, packed_rows, extra):
+    dest = ids_ref[...] * 12 + slot_ref[...]
+    gate = gate_ref[...].astype(F32) if scaled else jnp.ones(dest.shape, F32)
+    weight_a = jnp.zeros((rows, toks), F32)
+    weight_b = jnp.zeros((rows, toks), F32)
+    for k in range(dest.shape[0]):
+        d, g = dest[k : k + 1, :], gate[k : k + 1, :]
+        weight_a = jnp.where(d == id_a, g, weight_a)
+        weight_b = jnp.where(d == id_b, g, weight_b)
+    out_ref[:, :width] = dot(weight_a.astype(BF16), x_ref[...]).astype(BF16)
+    low = jnp.where(first, weight_b, 0.0).astype(BF16)
+    high = jnp.where(first, 0.0, weight_b).astype(BF16)
+    out_ref[:, width:] = dot(
+        jnp.concatenate([low, high], axis=1), halves_ref[...]
+    ).astype(BF16)
+
+
+def pack(ids_t, slot_t, gates_t, x, packed_rows, scaled):
     toks, width = x.shape
-    wide = width * 3 // 2 + extra
-    return pl.pallas_call(
-        pack_kernel,
+    wide = width * 3 // 2
+    return pl.pallas_call(
+        functools.partial(pack_kernel, scaled),
         grid=(packed_rows // CHUNK,),
         in_specs=[
-            pl.BlockSpec(dest_t.shape, lambda i: (0, 0)),
+            pl.BlockSpec(ids_t.shape, lambda i: (0, 0)),
+            pl.BlockSpec(slot_t.shape, lambda i: (0, 0)),
             pl.BlockSpec(gates_t.shape, lambda i: (0, 0)),
             pl.BlockSpec(x.shape, lambda i: (0, 0)),
         ],
         out_specs=pl.BlockSpec((CHUNK, wide), lambda i: (i, 0)),
         out_shape=jax.ShapeDtypeStruct((packed_rows, wide), BF16),
+        scratch_shapes=[pltpu.VMEM((2 * toks, width // 2), BF16)],
         compiler_params=pltpu.CompilerParams(vmem_limit_bytes=VMEM_LIMIT),
         cost_estimate=pl.CostEstimate(
             flops=2 * packed_rows * toks * width * 2,
             bytes_accessed=packed_rows * width * 3,
             transcendentals=0,
         ),
-    )(dest_t, gates_t, x)
+    )(ids_t, slot_t, gates_t, x)
 
 
 def sort_kernel(a_ref, b_ref, out_a, out_b):
@@ -159,7 +162,6 @@
     hidden_ref,
     pregate_ref,
     preup_ref,
-    scale_ref,
 ):
     packed = packed_ref.shape[0]
     width = rows_ref.shape[1]
@@ -168,18 +170,13 @@
     back_hidden = lax.dot_general(rows_ref[...], wd_ref[...], NT, preferred_element_type=F32)
     a = a_ref[...].astype(F32)
     b = b_ref[...].astype(F32)
-    extra = packed_ref[:, width + half :]
-    scale_ref[:packed, :] = extra[:, :1].astype(F32)
-    scale_ref[packed:, :] = dot(fold_masks(packed // 2, packed)[0], extra)[:, EXTRA // 2 : EXTRA // 2 + 1]
-    scale = scale_ref[...]
     sig = jax.nn.sigmoid(a)
     swish = a * sig
     hidden = swish * b
-    hidden_ref[...] = (hidden * scale).astype(BF16)
+    hidden_ref[...] = hidden.astype(BF16)
     slot_gate = jnp.sum(hidden * back_hidden, axis=1, keepdims=True).astype(BF16)
-    hidden_grad = scale * back_hidden
-    pregate = (hidden_grad * b * sig * (1.0 + a * (1.0 - sig))).astype(BF16)
-    preup = (hidden_grad * swish).astype(BF16)
+    pregate = (back_hidden * b * sig * (1.0 + a * (1.0 - sig))).astype(BF16)
+    preup = (back_hidden * swish).astype(BF16)
     pregate_ref[...] = pregate
     preup_ref[...] = preup
     slot_grad = (
@@ -209,6 +206,7 @@
     step = CHUNK * 3 // 2
     narrow = pl.BlockSpec((step, hidden_units), lambda i: (i, 0))
     packed_spec = pl.BlockSpec((CHUNK, wide), lambda i: (i, 0))
+    back_spec = pl.BlockSpec((CHUNK, wide + EXTRA), lambda i: (i, 0))
     return pl.pallas_call(
         expert_kernel,
         grid=(total // CHUNK,),
@@ -221,20 +219,19 @@
             pl.BlockSpec(weight_down.shape, lambda i: (0, 0)),
         ],
         out_specs=[
-            packed_spec,
+            back_spec,
             pl.BlockSpec((step, width), lambda i: (i, 0)),
             narrow,
             narrow,
             narrow,
         ],
         out_shape=[
-            jax.ShapeDtypeStruct((total, wide), BF16),
+            jax.ShapeDtypeStruct((total, wide + EXTRA), BF16),
             jax.ShapeDtypeStruct((rows, width), BF16),
             jax.ShapeDtypeStruct((rows, hidden_units), BF16),
             jax.ShapeDtypeStruct((rows, hidden_units), BF16),
             jax.ShapeDtypeStruct((rows, hidden_units), BF16),
         ],
-        scratch_shapes=[pltpu.VMEM((step, 1), F32)],
         compiler_params=pltpu.CompilerParams(vmem_limit_bytes=VMEM_LIMIT),
         cost_estimate=pl.CostEstimate(
             flops=6 * rows * width * hidden_units,
@@ -244,7 +241,7 @@
     )(packed, a, b, weight_gate, weight_up, weight_down)
 
 
-def combine_kernel(dest_ref, packed_ref, out_ref, gate_ref, acc_ref, gate_acc_ref):
+def combine_kernel(ids_ref, slot_ref, gate_ref, packed_ref, out_ref, terms_ref, acc_ref, term_acc_ref):
     step = pl.program_id(0)
     toks, width = out_ref.shape
     half = width // 2
@@ -255,69 +252,73 @@
     @pl.when(step == 0)
     def _():
         acc_ref[...] = jnp.zeros_like(acc_ref)
-        gate_acc_ref[...] = jnp.zeros_like(gate_acc_ref)
-
-    extra = packed_ref[:, width + half :]
-    lane = lax.broadcasted_iota(jnp.int32, (16, EXTRA), 1)
-    pick = lax.broadcasted_iota(jnp.int32, (16, EXTRA), 0) * (EXTRA // 2)
-    values = lax.dot_general(zero_one(lane == pick), extra, NT, preferred_element_type=F32)
-    value_a = values[0:1, :]
-    value_b = jnp.where(first[:1, :], values[1:2, :], 0.0)
-    column = lax.broadcasted_iota(jnp.int32, gate_acc_ref.shape, 1)
+        term_acc_ref[...] = jnp.zeros_like(term_acc_ref)
+
     hit_a = index < 0
     hit_b = index < 0
-    gates = gate_acc_ref[...]
-    for k in range(dest_ref.shape[1]):
-        d = dest_ref[:, k : k + 1]
-        here_a = d == id_a
-        here_b = d == id_b
-        hit_a = hit_a | here_a
-        hit_b = hit_b | here_b
-        found = jnp.where(here_a, value_a, jnp.where(here_b, value_b, 0.0))
-        gates += jnp.where(column == k, jnp.sum(found, axis=1, keepdims=True), 0.0)
-    gate_acc_ref[...] = gates
+    for k in range(ids_ref.shape[1]):
+        d = ids_ref[:, k : k + 1] * 12 + slot_ref[:, k : k + 1]
+        hit_a = hit_a | (d == id_a)
+        hit_b = hit_b | (d == id_b)
+    one_a = zero_one(hit_a)
+    low = zero_one(hit_b & first)
+    high = zero_one(hit_b & jnp.logical_not(first))
     rest = packed_ref[:, width : width + half]
-    one_a = zero_one(hit_a)
-
-    acc_ref[:, :half] += dot(one_a, packed_ref[:, :half]) + dot(zero_one(hit_b & first), rest)
-    acc_ref[:, half:] += dot(one_a, packed_ref[:, half:width]) + dot(
-        zero_one(hit_b & jnp.logical_not(first)), rest
-    )
+    acc_ref[:, :half] += dot(one_a, packed_ref[:, :half]) + dot(low, rest)
+    acc_ref[:, half:] += dot(one_a, packed_ref[:, half:width]) + dot(high, rest)
+
+    extra = packed_ref[:, width + half :]
+    lane = lax.broadcasted_iota(jnp.int32, (rows, EXTRA), 1)
+    pair = (lax.broadcasted_iota(jnp.int32, (rows, EXTRA), 0) + step * rows) >> 3
+    zero = jnp.zeros((), BF16)
+    value_a = jnp.where(lane == pair, extra[:, :1], zero)
+    value_b = jnp.where(lane == pair, extra[:, EXTRA // 2 : EXTRA // 2 + 1], zero)
+    term_acc_ref[...] += dot(one_a, value_a) + dot(low, value_b)
 
     @pl.when(step == pl.num_programs(0) - 1)
     def _():
         out_ref[...] = acc_ref[...].astype(BF16)
-        gate_ref[...] = gates[:, : gate_ref.shape[1]].astype(BF16)
-
-
-def combine(dest, packed, width):
-    toks, routes = dest.shape
+        terms = term_acc_ref[...]
+        expert_lane = lax.broadcasted_iota(jnp.int32, terms.shape, 1)
+        found = jnp.zeros(terms.shape, F32)
+        for k in range(ids_ref.shape[1]):
+            mine = jnp.where(expert_lane == ids_ref[:, k : k + 1], terms, 0.0)
+            term = jnp.sum(mine, axis=1, keepdims=True) / gate_ref[:, k : k + 1].astype(F32)
+            found = jnp.where(expert_lane == k, term, found)
+        row = lax.broadcasted_iota(jnp.int32, (16, EXTRA), 0)
+        column = lax.broadcasted_iota(jnp.int32, (16, EXTRA), 1)
+        turned = lax.dot_general(
+            zero_one(column == row), found.astype(BF16), NT, preferred_element_type=F32
+        )
+        terms_ref[...] = turned[: terms_ref.shape[0], :].astype(BF16)
+
+
+def combine(ids, slots, gates, packed, width):
+    toks, routes = ids.shape
     total, wide = packed.shape
+    table = pl.BlockSpec(ids.shape, lambda i: (0, 0))
     return pl.pallas_call(
         combine_kernel,
         grid=(total // CHUNK,),
-        in_specs=[
-            pl.BlockSpec(dest.shape, lambda i: (0, 0)),
-            pl.BlockSpec((CHUNK, wide), lambda i: (i, 0)),
-        ],
+        in_specs=[table, table, table, pl.BlockSpec((CHUNK, wide), lambda i: (i, 0))],
         out_specs=[
             pl.BlockSpec((toks, width), lambda i: (0, 0)),
-            pl.BlockSpec((toks, routes), lambda i: (0, 0)),
+            pl.BlockSpec((routes, toks), lambda i: (0, 0)),
         ],
         out_shape=[
             jax.ShapeDtypeStruct((toks, width), BF16),
-            jax.ShapeDtypeStruct((toks, routes), BF16),
+            jax.ShapeDtypeStruct((routes, toks), BF16),
         ],
         scratch_shapes=[pltpu.VMEM((toks, width), F32), pltpu.VMEM((toks, EXTRA), F32)],
         compiler_params=pltpu.CompilerParams(vmem_limit_bytes=VMEM_LIMIT),
         cost_estimate=pl.CostEstimate(
             flops=2 * total * toks * width * 2, bytes_accessed=total * wide * 2, transcendentals=0
         ),
-    )(dest, packed)
-
-
-def exchange(x):
-    return lax.all_to_all(x, AXES, split_axis=0, concat_axis=0, tiled=True)
+    )(ids, slots, gates, packed)
+
+
+def exchange(x, axes):
+    return lax.all_to_all(x, axes, split_axis=0, concat_axis=0, tiled=True)
 
 
 def body(
@@ -334,19 +335,17 @@
 ):
     experts = lax.axis_size("group") * lax.axis_size("member")
     width = tokens.shape[1]
-    pair_rows = saved_gate.shape[1] // experts
     packed_rows = experts * 8
-    dest = expert_ids * pair_rows + pair_slot
-    dest_t = expert_ids.T * pair_rows + pair_slot.T
-
-    gates_t = gate_weights.T.astype(F32)
-    here_grads = exchange(pack(dest_t, gates_t, grad_out, packed_rows, EXTRA))
-    here_tokens = exchange(pack(dest_t, gates_t, tokens, packed_rows, 0))
+    routing = (expert_ids.T, pair_slot.T, gate_weights.T)
+
+    here_grads = exchange(pack(*routing, grad_out, packed_rows, True), AXES)
+    here_tokens = exchange(pack(*routing, tokens, packed_rows, False), AXES)
     a, b = sort_rows(saved_gate[0], saved_up[0])
     back, grad_rows, hidden, pregate, preup = expert(
         here_grads, a, b, weight_gate[0], weight_up[0], weight_down[0]
     )
-    back_packed = exchange(back)
+    back, here_tokens = lax.optimization_barrier((back, here_tokens))
+    back_packed = exchange(back, AXES)
 
     token_rows = unpack(here_tokens)
     over_rows = (((0,), (0,)), ((), ()))
@@ -354,10 +353,10 @@
     gate_total = lax.dot_general(token_rows, pregate, over_rows, preferred_element_type=F32)
     up_total = lax.dot_general(token_rows, preup, over_rows, preferred_element_type=F32)
 
-    grad_tokens, grad_gates = combine(dest, back_packed, width)
+    grad_tokens, grad_gates = combine(expert_ids, pair_slot, gate_weights, back_packed, width)
     return (
         grad_tokens,
-        grad_gates,
+        grad_gates.T,
         gate_total[None].astype(BF16),
         up_total[None].astype(BF16),
         down_total[None].astype(BF16),

time: 284 us -> 277 us (0.975)
  waiting for transfers between devices: 166 us -> 162 us
    all_to_all x3, waiting for transfers between devices: 166 us -> 162 us  [exchange(): return lax.all_to_all(x, axes, split_axis=0, concat_axis=0, tiled=True)]
    dot_general x1, matrix products: 9.71 us -> 6.53 us  [body(): lax.dot_general(token_rows, pregate, over_rows, preferred_element_type=F32)]
    dot_general x1, matrix products: 6.53 us -> 9.71 us  [body(): lax.dot_general(token_rows, preup, over_rows, preferred_element_type=F32)]
  transfers between devices with their start and end apart: 3 -> 3, of which waited for: 3 -> 3; matrix products, arithmetic and copies ran while one was open for 8% -> 9% of each run, Pallas kernels for 17% -> 17%
where the time goes in v3:
time: 277 us
  waiting for transfers between devices  162 us (58%)
  Pallas kernels  59.6 us (22%)
  starting transfers between devices  29.1 us (11%)
  matrix products  22.7 us (8%)
    all_to_all x3, waiting for transfers between devices, exchange(): return lax.all_to_all(x, axes, split_axis=0, concat_axis=0, tiled=True)  162 us
    all_to_all x3, starting transfers between devices, exchange(): return lax.all_to_all(x, axes, split_axis=0, concat_axis=0, tiled=True)  29.1 us
    pallas_call x1, Pallas kernels, expert(): pl.pallas_call(expert_kernel, grid=(total // CHUNK,), in_specs=[packed_sp...  28.6 us
    pallas_call x2, Pallas kernels, pack(): pl.pallas_call(functools.partial(pack_kernel, scaled), grid=(packed_rows...  10.7 us
    dot_general x1, matrix products, body(): lax.dot_general(token_rows, preup, over_rows, preferred_element_type=F32)  9.71 us
    pallas_call x1, Pallas kernels, combine(): pl.pallas_call(combine_kernel, grid=(total // CHUNK,), in_specs=[table, t...  7.89 us
    dot_general x1, matrix products, body(): lax.dot_general(token_rows, pregate, over_rows, preferred_element_type=F32)  6.53 us
    dot_general x1, matrix products, body(): lax.dot_general(hidden, grad_rows, over_rows, preferred_element_type=F32)  6.47 us
  transfers between devices with their start and end apart: 3, of which 3 were waited for; matrix products, arithmetic and copies ran while one was open for 9% of the time, Pallas kernels for 17%

profile of v3, /device:TPU:1, one launch (start us, length us, event | category | flops | bytes accessed | tf_op | source)
XLA Modules:
  0.0 276.5 jit_solution(787070118649635714)
XLA Ops:
  0.6 5.4 %shard_map.137 = bf16[1024,3072]{1,0:T(8,128)(2,1)} custom-call(s32[8,128]{1,0:T(8,128)} %bitcast.30, s32[8,128]{1,0:T(8,128)} %bitcast.32, bf16[8,128]{1,0:T(8,128)(2,1)} %bitcast.34, bf16[128,2048]{1,0:T(8,128)(2,1)} %x_ref.2), custom_call_target="tpu_custom_call" | custom-call | flops 1073741824 | bytes 6291456 | tf_op jit(solution)/shard_map/pallas_call | solution.py:69
  6.0 11.9 %all-to-all-start = ((bf16[128,8,3072]{2,1,0:T(8,128)(2,1)}), bf16[128,8,3072]{2,1,0:T(8,128)(2,1)}, u32[]{:S(2)}, u32[]{:S(2)}) async-start(bf16[128,8,3072]{2,1,0:T(8,128)(2,1)} %bitcast.28), calls=%async_computation | async-start | bytes 12582912 | tf_op jit(solution)/shard_map/all_to_all | solution.py:321
  18.0 5.3 %shard_map.140 = bf16[1024,3072]{1,0:T(8,128)(2,1)} custom-call(s32[8,128]{1,0:T(8,128)} %bitcast.31, s32[8,128]{1,0:T(8,128)} %bitcast.33, bf16[8,128]{1,0:T(8,128)(2,1)} %bitcast.35, bf16[128,2048]{1,0:T(8,128)(2,1)} %x_ref.3), custom_call_target="tpu_custom_call" | custom-call | flops 1073741824 | bytes 6291456 | tf_op jit(solution)/shard_map/pallas_call | solution.py:69
  23.3 71.5 %all-to-all-done = bf16[128,8,3072]{2,1,0:T(8,128)(2,1)} async-done(((bf16[128,8,3072]{2,1,0:T(8,128)(2,1)}), bf16[128,8,3072]{2,1,0:T(8,128)(2,1)}, u32[]{:S(2)}, u32[]{:S(2)}) %all-to-all-start) | async-done | bytes 6291488 | tf_op jit(solution)/shard_map/all_to_all | solution.py:321
  94.8 8.6 %all-to-all-start.1 = ((bf16[128,8,3072]{2,1,0:T(8,128)(2,1)}), bf16[128,8,3072]{2,1,0:T(8,128)(2,1)}, u32[]{:S(2)}, u32[]{:S(2)}) async-start(bf16[128,8,3072]{2,1,0:T(8,128)(2,1)} %bitcast.27), calls=%async_computation.1 | async-start | bytes 12582912 | tf_op jit(solution)/shard_map/all_to_all | solution.py:321
  103.4 6.0 %shard_map.138 = (bf16[1536,768]{1,0:T(8,128)(2,1)}, bf16[1536,768]{1,0:T(8,128)(2,1)}) custom-call(bf16[1536,768]{1,0:T(8,128)(2,1)} %bitcast.39, bf16[1536,768]{1,0:T(8,128)(2,1)} %bitcast.40), custom_call_target="tpu_custom_call" | custom-call | flops 1811939328 | bytes 9437184 | tf_op jit(solution)/shard_map/pallas_call | solution.py:106
  109.4 28.6 %shard_map.139 = (bf16[1024,3200]{1,0:T(8,128)(2,1)}, bf16[1536,2048]{1,0:T(8,128)(2,1)}, bf16[1536,768]{1,0:T(8,128)(2,1)}, bf16[1536,768]{1,0:T(8,128)(2,1)}, bf16[1536,768]{1,0:T(8,128)(2,1)}) custom-call(bf16[1024,3072]{1,0:T(8,128)(2,1)} %bitcast.4.packed_ref, bf16[1536,768]{1,0:T(8,128)(2,1)} %get-tuple-element.16.a_ref, ...), custom_call_target="tpu_custom_call" | custom-call | flops 14495514624 | bytes 18874368 | tf_op jit(solution)/shard_map/pallas_call | solution.py:210
  138.0 42.3 %all-to-all-done.1 = bf16[128,8,3072]{2,1,0:T(8,128)(2,1)} async-done(((bf16[128,8,3072]{2,1,0:T(8,128)(2,1)}), bf16[128,8,3072]{2,1,0:T(8,128)(2,1)}, u32[]{:S(2)}, u32[]{:S(2)}) %all-to-all-start.1) | async-done | bytes 6291488 | tf_op jit(solution)/shard_map/all_to_all | solution.py:321
  180.2 8.6 %all-to-all-start.2 = ((bf16[128,8,3200]{2,1,0:T(8,128)(2,1)}), bf16[128,8,3200]{2,1,0:T(8,128)(2,1)}, u32[]{:S(2)}, u32[]{:S(2)}) async-start(bf16[128,8,3200]{2,1,0:T(8,128)(2,1)} %bitcast.29), calls=%async_computation.2 | async-start | bytes 13107200 | tf_op jit(solution)/shard_map/all_to_all | solution.py:321
  188.9 0.0 copy-done.1
  188.9 0.7 copy.15.ids_ref
  189.6 0.0 copy-done.2
  189.6 0.7 copy.16.slot_ref
  190.3 0.0 copy-done.3
  190.3 0.7 copy.17.gate_ref
  191.0 6.4 %shard_map.142 = bf16[1536,2048]{1,0:T(8,128)(2,1)} custom-call(bf16[1024,3072]{1,0:T(8,128)(2,1)} %bitcast.11.packed_ref), custom_call_target="tpu_custom_call" | custom-call | flops 1073741824 | bytes 12582912 | tf_op jit(solution)/shard_map/pallas_call | solution.py:140
  197.5 0.0 copy-done.6
  197.5 0.0 slice-start
  197.5 9.7 %fusion.1 = bf16[1,2048,768]{2,1,0:T(8,128)(2,1)} fusion(bf16[1536,2048]{1,0:T(8,128)(2,1)} %shard_map.142, bf16[1536,768]{1,0:T(8,128)(2,1)S(1)} %copy-done.6), kind=kOutput, calls=%fused_computation.4 | convolution fusion | flops 4833411072 | bytes 11796480 | tf_op jit(solution)/shard_map/dot_general | solution.py:354
  207.2 6.5 %fusion = bf16[1,2048,768]{2,1,0:T(8,128)(2,1)} fusion(bf16[1536,2048]{1,0:T(8,128)(2,1)S(1)} %copy-done, bf16[1536,768]{1,0:T(8,128)(2,1)S(1)} %copy-done.5), kind=kOutput, calls=%fused_computation.3 | convolution fusion | flops 4833411072 | bytes 11796480 | tf_op jit(solution)/shard_map/dot_general | solution.py:353
  213.8 0.0 slice-done.1
  213.8 6.5 %fusion.2 = bf16[1,768,2048]{2,1,0:T(8,128)(2,1)} fusion(bf16[1536,768]{1,0:T(8,128)(2,1)S(1)} %copy-done.4, bf16[1536,2048]{1,0:T(8,128)(2,1)S(1)} %bitcast.43), kind=kOutput, calls=%fused_computation.5 | convolution fusion | flops 4833411072 | bytes 11796480 | tf_op jit(solution)/shard_map/dot_general | solution.py:352
  220.2 48.4 %all-to-all-done.2 = bf16[128,8,3200]{2,1,0:T(8,128)(2,1)} async-done(((bf16[128,8,3200]{2,1,0:T(8,128)(2,1)}), bf16[128,8,3200]{2,1,0:T(8,128)(2,1)}, u32[]{:S(2)}, u32[]{:S(2)}) %all-to-all-start.2) | async-done | bytes 6553632 | tf_op jit(solution)/shard_map/all_to_all | solution.py:321
  268.6 7.9 %shard_map.141 = (bf16[128,2048]{1,0:T(8,128)(2,1)}, bf16[8,128]{1,0:T(8,128)(2,1)}) custom-call(s32[128,8]{1,0:T(8,128)} %copy.15.ids_ref, s32[128,8]{1,0:T(8,128)} %copy.16.slot_ref, bf16[128,8]{1,0:T(8,128)(2,1)} %copy.17.gate_ref, bf16[1024,3200]{1,0:T(8,128)(2,1)} %bitcast.13.packed_ref), custom_call_target="tpu_custom_call" | custom-call | flops 1073741824 | bytes 6553600 | tf_op jit(solution)/shard_map/pallas_call | solution.py:300
  (13 shorter events, 0.0 us)
Async XLA Ops:
  6.0 88.8 %all-to-all-start = ((bf16[128,8,3072]{2,1,0:T(8,128)(2,1)}), bf16[128,8,3072]{2,1,0:T(8,128)(2,1)}, u32[]{:S(2)}, u32[]{:S(2)}) async-start(bf16[128,8,3072]{2,1,0:T(8,128)(2,1)} %bitcast.28), calls=%async_computation | async-start | bytes 12582912 | tf_op jit(solution)/shard_map/all_to_all | solution.py:321
  94.8 85.4 %all-to-all-start.1 = ((bf16[128,8,3072]{2,1,0:T(8,128)(2,1)}), bf16[128,8,3072]{2,1,0:T(8,128)(2,1)}, u32[]{:S(2)}, u32[]{:S(2)}) async-start(bf16[128,8,3072]{2,1,0:T(8,128)(2,1)} %bitcast.27), calls=%async_computation.1 | async-start | bytes 12582912 | tf_op jit(solution)/shard_map/all_to_all | solution.py:321
  180.2 8.6 %copy-start.1 = (s32[128,8]{0,1:T(8,128)S(1)}, s32[128,8]{0,1:T(8,128)}, u32[]{:S(2)}) copy-start(s32[128,8]{0,1:T(8,128)} %param.12) | copy-start | bytes 12292
  180.2 9.4 %copy-start.2 = (s32[128,8]{0,1:T(8,128)S(1)}, s32[128,8]{0,1:T(8,128)}, u32[]{:S(2)}) copy-start(s32[128,8]{0,1:T(8,128)} %param.13) | copy-start | bytes 12292
  180.2 10.1 %copy-start.3 = (bf16[128,8]{0,1:T(8,128)(2,1)S(1)}, bf16[128,8]{0,1:T(8,128)(2,1)}, u32[]{:S(2)}) copy-start(bf16[128,8]{0,1:T(8,128)(2,1)} %param.14) | copy-start | bytes 6148
  180.2 88.4 %all-to-all-start.2 = ((bf16[128,8,3200]{2,1,0:T(8,128)(2,1)}), bf16[128,8,3200]{2,1,0:T(8,128)(2,1)}, u32[]{:S(2)}, u32[]{:S(2)}) async-start(bf16[128,8,3200]{2,1,0:T(8,128)(2,1)} %bitcast.29), calls=%async_computation.2 | async-start | bytes 13107200 | tf_op jit(solution)/shard_map/all_to_all | solution.py:321
  191.0 6.4 %copy-start.6 = (bf16[1536,768]{1,0:T(8,128)(2,1)S(1)}, bf16[1536,768]{1,0:T(8,128)(2,1)}, u32[]{:S(2)}) copy-start(bf16[1536,768]{1,0:T(8,128)(2,1)} %get-tuple-element.24) | copy-start | bytes 7077892
  197.5 9.7 %copy-start = (bf16[1536,2048]{1,0:T(8,128)(2,1)S(1)}, bf16[1536,2048]{1,0:T(8,128)(2,1)}, u32[]{:S(2)}) copy-start(bf16[1536,2048]{1,0:T(8,128)(2,1)} %shard_map.142) | copy-start | bytes 18874372
  197.5 9.7 %copy-start.5 = (bf16[1536,768]{1,0:T(8,128)(2,1)S(1)}, bf16[1536,768]{1,0:T(8,128)(2,1)}, u32[]{:S(2)}) copy-start(bf16[1536,768]{1,0:T(8,128)(2,1)} %get-tuple-element.23) | copy-start | bytes 7077892
  197.5 16.3 %slice-start = ((s8[6291456]{0:T(1024)(128)(4,1)}), s8[4194304]{0:T(1024)(128)(4,1)S(1)}, s32[]{:S(2)}) async-start(s8[6291456]{0:T(1024)(128)(4,1)} %bitcast.42), calls=%async_computation.3 | async-start | bytes 8388608
  207.2 6.5 %slice-start.1 = ((s8[6291456]{0:T(1024)(128)(4,1)}), s8[2097152]{0:T(1024)(128)(4,1)S(1)}, s32[]{:S(2)}) async-start(s8[6291456]{0:T(1024)(128)(4,1)} %bitcast.42), calls=%async_computation.4 | async-start | bytes 4194304
  207.2 6.5 %copy-start.4 = (bf16[1536,768]{1,0:T(8,128)(2,1)S(1)}, bf16[1536,768]{1,0:T(8,128)(2,1)}, u32[]{:S(2)}) copy-start(bf16[1536,768]{1,0:T(8,128)(2,1)} %get-tuple-element.25) | copy-start | bytes 7077892

commit v4 on v3

--- a/solution.py
+++ b/solution.py
@@ -11,6 +11,8 @@
 BF16 = jnp.bfloat16
 AXES = ("group", "member")
 CHUNK = 256
+BLOCK = 128
+LOAD = 256
 NT = (((1,), (1,)), ((), ()))
 VMEM_LIMIT = 56 * 1024 * 1024
 
@@ -35,32 +37,38 @@
     return jnp.where(lane < EXTRA // 2, a, b).astype(BF16)
 
 
-def pack_kernel(scaled, ids_ref, slot_ref, gate_ref, x_ref, out_ref, halves_ref):
-    rows, toks = out_ref.shape[0], x_ref.shape[0]
-    width = x_ref.shape[1]
+def pack_kernel(scaled, ids_ref, slot_ref, gate_ref, x_ref, out_ref, halves_ref, made_ref, sems):
+    toks, width = x_ref.shape
     half = width // 2
-
-    @pl.when(pl.program_id(0) == 0)
-    def _():
-        halves_ref[:toks, :] = x_ref[:, :half]
-        halves_ref[toks:, :] = x_ref[:, half:]
-
-    index = lax.broadcasted_iota(jnp.int32, (rows, toks), 0) + pl.program_id(0) * rows
-    id_a, id_b, first = packed_ids(index)
+    rows = BLOCK
+    halves_ref[:toks, :] = x_ref[:, :half]
+    halves_ref[toks:, :] = x_ref[:, half:]
     dest = ids_ref[...] * 12 + slot_ref[...]
     gate = gate_ref[...].astype(F32) if scaled else jnp.ones(dest.shape, F32)
-    weight_a = jnp.zeros((rows, toks), F32)
-    weight_b = jnp.zeros((rows, toks), F32)
-    for k in range(dest.shape[0]):
-        d, g = dest[k : k + 1, :], gate[k : k + 1, :]
-        weight_a = jnp.where(d == id_a, g, weight_a)
-        weight_b = jnp.where(d == id_b, g, weight_b)
-    out_ref[:, :width] = dot(weight_a.astype(BF16), x_ref[...]).astype(BF16)
-    low = jnp.where(first, weight_b, 0.0).astype(BF16)
-    high = jnp.where(first, 0.0, weight_b).astype(BF16)
-    out_ref[:, width:] = dot(
-        jnp.concatenate([low, high], axis=1), halves_ref[...]
-    ).astype(BF16)
+    copies = []
+    for block in range(made_ref.shape[0] // rows):
+        index = lax.broadcasted_iota(jnp.int32, (rows, 1), 0) + block * rows
+        id_a, id_b, first = packed_ids(index)
+        id_low = jnp.where(first, id_b, -1)
+        id_high = jnp.where(first, -1, id_b)
+        weight_a = jnp.zeros((rows, toks), F32)
+        low = jnp.zeros((rows, toks), F32)
+        high = jnp.zeros((rows, toks), F32)
+        for k in range(dest.shape[0]):
+            d, g = dest[k : k + 1, :], gate[k : k + 1, :]
+            weight_a = jnp.where(d == id_a, g, weight_a)
+            low = jnp.where(d == id_low, g, low)
+            high = jnp.where(d == id_high, g, high)
+        here = pl.ds(block * rows, rows)
+        made_ref[here, :width] = dot(weight_a.astype(BF16), x_ref[...]).astype(BF16)
+        made_ref[here, width:] = dot(
+            jnp.concatenate([low, high], axis=1).astype(BF16), halves_ref[...]
+        ).astype(BF16)
+        copy = pltpu.make_async_copy(made_ref.at[here, :], out_ref.at[here, :], sems.at[block])
+        copy.start()
+        copies.append(copy)
+    for copy in copies:
+        copy.wait()
 
 
 def pack(ids_t, slot_t, gates_t, x, packed_rows, scaled):
@@ -68,16 +76,13 @@
     wide = width * 3 // 2
     return pl.pallas_call(
         functools.partial(pack_kernel, scaled),
-        grid=(packed_rows // CHUNK,),
-        in_specs=[
-            pl.BlockSpec(ids_t.shape, lambda i: (0, 0)),
-            pl.BlockSpec(slot_t.shape, lambda i: (0, 0)),
-            pl.BlockSpec(gates_t.shape, lambda i: (0, 0)),
-            pl.BlockSpec(x.shape, lambda i: (0, 0)),
-        ],
-        out_specs=pl.BlockSpec((CHUNK, wide), lambda i: (i, 0)),
+        out_specs=pl.BlockSpec(memory_space=pl.ANY),
         out_shape=jax.ShapeDtypeStruct((packed_rows, wide), BF16),
-        scratch_shapes=[pltpu.VMEM((2 * toks, width // 2), BF16)],
+        scratch_shapes=[
+            pltpu.VMEM((2 * toks, width // 2), BF16),
+            pltpu.VMEM((packed_rows, wide), BF16),
+            pltpu.SemaphoreType.DMA((packed_rows // BLOCK,)),
+        ],
         compiler_params=pltpu.CompilerParams(vmem_limit_bytes=VMEM_LIMIT),
         cost_estimate=pl.CostEstimate(
             flops=2 * packed_rows * toks * width * 2,
@@ -241,75 +246,85 @@
     )(packed, a, b, weight_gate, weight_up, weight_down)
 
 
-def combine_kernel(ids_ref, slot_ref, gate_ref, packed_ref, out_ref, terms_ref, acc_ref, term_acc_ref):
-    step = pl.program_id(0)
+def combine_kernel(
+    ids_ref, slot_ref, gate_ref, packed_ref, out_ref, terms_ref, here_ref, masks_ref, sems
+):
     toks, width = out_ref.shape
     half = width // 2
-    rows = packed_ref.shape[0]
-    index = lax.broadcasted_iota(jnp.int32, (toks, rows), 1) + step * rows
-    id_a, id_b, first = packed_ids(index)
-
-    @pl.when(step == 0)
-    def _():
-        acc_ref[...] = jnp.zeros_like(acc_ref)
-        term_acc_ref[...] = jnp.zeros_like(term_acc_ref)
-
-    hit_a = index < 0
-    hit_b = index < 0
-    for k in range(ids_ref.shape[1]):
-        d = ids_ref[:, k : k + 1] * 12 + slot_ref[:, k : k + 1]
-        hit_a = hit_a | (d == id_a)
-        hit_b = hit_b | (d == id_b)
-    one_a = zero_one(hit_a)
-    low = zero_one(hit_b & first)
-    high = zero_one(hit_b & jnp.logical_not(first))
-    rest = packed_ref[:, width : width + half]
-    acc_ref[:, :half] += dot(one_a, packed_ref[:, :half]) + dot(low, rest)
-    acc_ref[:, half:] += dot(one_a, packed_ref[:, half:width]) + dot(high, rest)
-
-    extra = packed_ref[:, width + half :]
-    lane = lax.broadcasted_iota(jnp.int32, (rows, EXTRA), 1)
-    pair = (lax.broadcasted_iota(jnp.int32, (rows, EXTRA), 0) + step * rows) >> 3
-    zero = jnp.zeros((), BF16)
-    value_a = jnp.where(lane == pair, extra[:, :1], zero)
-    value_b = jnp.where(lane == pair, extra[:, EXTRA // 2 : EXTRA // 2 + 1], zero)
-    term_acc_ref[...] += dot(one_a, value_a) + dot(low, value_b)
-
-    @pl.when(step == pl.num_programs(0) - 1)
-    def _():
-        out_ref[...] = acc_ref[...].astype(BF16)
-        terms = term_acc_ref[...]
-        expert_lane = lax.broadcasted_iota(jnp.int32, terms.shape, 1)
-        found = jnp.zeros(terms.shape, F32)
-        for k in range(ids_ref.shape[1]):
-            mine = jnp.where(expert_lane == ids_ref[:, k : k + 1], terms, 0.0)
-            term = jnp.sum(mine, axis=1, keepdims=True) / gate_ref[:, k : k + 1].astype(F32)
-            found = jnp.where(expert_lane == k, term, found)
-        row = lax.broadcasted_iota(jnp.int32, (16, EXTRA), 0)
-        column = lax.broadcasted_iota(jnp.int32, (16, EXTRA), 1)
-        turned = lax.dot_general(
-            zero_one(column == row), found.astype(BF16), NT, preferred_element_type=F32
-        )
-        terms_ref[...] = turned[: terms_ref.shape[0], :].astype(BF16)
+    total = here_ref.shape[0]
+    rows = LOAD
+    copies = []
+    for block in range(total // rows):
+        at = pl.ds(block * rows, rows)
+        copy = pltpu.make_async_copy(packed_ref.at[at, :], here_ref.at[at, :], sems.at[block])
+        copy.start()
+        copies.append(copy)
+
+    ids = ids_ref[...]
+    dest = ids * 12 + slot_ref[...]
+    columns = [jnp.broadcast_to(dest[:, k : k + 1], (toks, 128)) for k in range(dest.shape[1])]
+    for start in range(0, total, 128):
+        index = lax.broadcasted_iota(jnp.int32, (1, 128), 1) + start
+        id_a, id_b, first = packed_ids(index)
+        id_low = jnp.where(first, id_b, -1)
+        id_high = jnp.where(first, -1, id_b)
+        hits = [column == id_a for column in columns]
+        lows = [column == id_low for column in columns]
+        highs = [column == id_high for column in columns]
+        for n, found in enumerate((hits, lows, highs)):
+            mask = functools.reduce(jnp.logical_or, found)
+            masks_ref[n * toks : (n + 1) * toks, start : start + 128] = zero_one(mask)
+
+    terms = jnp.zeros((toks, EXTRA), F32)
+    left = jnp.zeros((toks, half), F32)
+    right = jnp.zeros((toks, half), F32)
+    for block, copy in enumerate(copies):
+        copy.wait()
+        at = slice(block * rows, (block + 1) * rows)
+        one_a = masks_ref[:toks, at]
+        folded = dot(masks_ref[toks:, at], here_ref[at, width : width + half])
+        left += dot(one_a, here_ref[at, :half]) + folded[:toks, :]
+        right += dot(one_a, here_ref[at, half:width]) + folded[toks:, :]
+        extra = here_ref[at, width + half :]
+        lane = lax.broadcasted_iota(jnp.int32, (rows, EXTRA), 1)
+        pair = (lax.broadcasted_iota(jnp.int32, (rows, EXTRA), 0) + block * rows) >> 3
+        zero = jnp.zeros((), BF16)
+        value_a = jnp.where(lane == pair, extra[:, :1], zero)
+        value_b = jnp.where(lane == pair, extra[:, EXTRA // 2 : EXTRA // 2 + 1], zero)
+        terms += dot(one_a, value_a) + dot(masks_ref[toks : 2 * toks, at], value_b)
+    out_ref[:, :half] = left.astype(BF16)
+    out_ref[:, half:] = right.astype(BF16)
+
+    expert_lane = lax.broadcasted_iota(jnp.int32, terms.shape, 1)
+    found = jnp.zeros(terms.shape, F32)
+    for k in range(ids.shape[1]):
+        mine = jnp.where(expert_lane == ids[:, k : k + 1], terms, 0.0)
+        term = jnp.sum(mine, axis=1, keepdims=True) / gate_ref[:, k : k + 1].astype(F32)
+        found = jnp.where(expert_lane == k, term, found)
+    row = lax.broadcasted_iota(jnp.int32, (16, EXTRA), 0)
+    column = lax.broadcasted_iota(jnp.int32, (16, EXTRA), 1)
+    turned = lax.dot_general(
+        zero_one(column == row), found.astype(BF16), NT, preferred_element_type=F32
+    )
+    terms_ref[...] = turned[: terms_ref.shape[0], :].astype(BF16)
 
 
 def combine(ids, slots, gates, packed, width):
     toks, routes = ids.shape
     total, wide = packed.shape
-    table = pl.BlockSpec(ids.shape, lambda i: (0, 0))
+    table = pl.BlockSpec(memory_space=pltpu.VMEM)
     return pl.pallas_call(
         combine_kernel,
-        grid=(total // CHUNK,),
-        in_specs=[table, table, table, pl.BlockSpec((CHUNK, wide), lambda i: (i, 0))],
-        out_specs=[
-            pl.BlockSpec((toks, width), lambda i: (0, 0)),
-            pl.BlockSpec((routes, toks), lambda i: (0, 0)),
-        ],
+        in_specs=[table, table, table, pl.BlockSpec(memory_space=pl.ANY)],
         out_shape=[
             jax.ShapeDtypeStruct((toks, width), BF16),
             jax.ShapeDtypeStruct((routes, toks), BF16),
         ],
-        scratch_shapes=[pltpu.VMEM((toks, width), F32), pltpu.VMEM((toks, EXTRA), F32)],
+        scratch_shapes=[
+            pltpu.VMEM((total, wide), BF16),
+            pltpu.VMEM((3 * toks, total), BF16),
+            pltpu.SemaphoreType.DMA((total // LOAD,)),
+        ],
         compiler_params=pltpu.CompilerParams(vmem_limit_bytes=VMEM_LIMIT),
         cost_estimate=pl.CostEstimate(
             flops=2 * total * toks * width * 2, bytes_accessed=total * wide * 2, transcendentals=0

time: 277 us -> 274 us (0.989)
  Pallas kernels: 59.6 us -> 55 us
    pallas_call x3, Pallas kernels: 18.6 us -> 14 us  [the longest x2 8.49 us: pack(): pl.pallas_call(functools.partial(pack_kernel, scaled), out_specs=pl.Block...]
where the time goes in v4:
time: 274 us; the launch traced here: 273 us
  waiting for transfers between devices  163 us (59%)
  Pallas kernels  55 us (20%)
  starting transfers between devices  29.1 us (11%)
  matrix products  22.7 us (8%)
    all_to_all x3, waiting for transfers between devices, exchange(): return lax.all_to_all(x, axes, split_axis=0, concat_axis=0, tiled=True)  163 us
    all_to_all x3, starting transfers between devices, exchange(): return lax.all_to_all(x, axes, split_axis=0, concat_axis=0, tiled=True)  29.1 us
    pallas_call x1, Pallas kernels, expert(): pl.pallas_call(expert_kernel, grid=(total // CHUNK,), in_specs=[packed_sp...  28.5 us
    dot_general x1, matrix products, body(): lax.dot_general(token_rows, preup, over_rows, preferred_element_type=F32)  9.71 us
    pallas_call x2, Pallas kernels, pack(): pl.pallas_call(functools.partial(pack_kernel, scaled), out_specs=pl.Block...  8.49 us
    dot_general x1, matrix products, body(): lax.dot_general(token_rows, pregate, over_rows, preferred_element_type=F32)  6.53 us
    dot_general x1, matrix products, body(): lax.dot_general(hidden, grad_rows, over_rows, preferred_element_type=F32)  6.47 us
    pallas_call x1, Pallas kernels, unpack(): pl.pallas_call(unpack_into, grid=(total // CHUNK,), in_specs=[pl.BlockSpe...  6.44 us
  transfers between devices with their start and end apart: 3, of which 3 were waited for; matrix products, arithmetic and copies ran while one was open for 9% of the time, Pallas kernels for 17%

profile of v4, /device:TPU:1, one launch (start us, length us, event | category | flops | bytes accessed | tf_op | source)
XLA Modules:
  0.0 273.1 jit_solution(11177775560984074084)
XLA Ops:
  0.6 4.2 %shard_map.137 = bf16[1024,3072]{1,0:T(8,128)(2,1)} custom-call(s32[8,128]{1,0:T(8,128)} %bitcast.30, s32[8,128]{1,0:T(8,128)} %bitcast.32, bf16[8,128]{1,0:T(8,128)(2,1)} %bitcast.34, bf16[128,2048]{1,0:T(8,128)(2,1)} %x_ref.2), custom_call_target="tpu_custom_call" | custom-call | flops 1073741824 | bytes 6291456 | tf_op jit(solution)/shard_map/pallas_call | solution.py:77
  4.9 11.9 %all-to-all-start = ((bf16[128,8,3072]{2,1,0:T(8,128)(2,1)}), bf16[128,8,3072]{2,1,0:T(8,128)(2,1)}, u32[]{:S(2)}, u32[]{:S(2)}) async-start(bf16[128,8,3072]{2,1,0:T(8,128)(2,1)} %bitcast.28), calls=%async_computation | async-start | bytes 12582912 | tf_op jit(solution)/shard_map/all_to_all | solution.py:336
  16.8 4.3 %shard_map.140 = bf16[1024,3072]{1,0:T(8,128)(2,1)} custom-call(s32[8,128]{1,0:T(8,128)} %bitcast.31, s32[8,128]{1,0:T(8,128)} %bitcast.33, bf16[8,128]{1,0:T(8,128)(2,1)} %bitcast.35, bf16[128,2048]{1,0:T(8,128)(2,1)} %x_ref.3), custom_call_target="tpu_custom_call" | custom-call | flops 1073741824 | bytes 6291456 | tf_op jit(solution)/shard_map/pallas_call | solution.py:77
  21.1 72.6 %all-to-all-done = bf16[128,8,3072]{2,1,0:T(8,128)(2,1)} async-done(((bf16[128,8,3072]{2,1,0:T(8,128)(2,1)}), bf16[128,8,3072]{2,1,0:T(8,128)(2,1)}, u32[]{:S(2)}, u32[]{:S(2)}) %all-to-all-start) | async-done | bytes 6291488 | tf_op jit(solution)/shard_map/all_to_all | solution.py:336
  93.6 8.6 %all-to-all-start.1 = ((bf16[128,8,3072]{2,1,0:T(8,128)(2,1)}), bf16[128,8,3072]{2,1,0:T(8,128)(2,1)}, u32[]{:S(2)}, u32[]{:S(2)}) async-start(bf16[128,8,3072]{2,1,0:T(8,128)(2,1)} %bitcast.27), calls=%async_computation.1 | async-start | bytes 12582912 | tf_op jit(solution)/shard_map/all_to_all | solution.py:336
  102.2 6.0 %shard_map.138 = (bf16[1536,768]{1,0:T(8,128)(2,1)}, bf16[1536,768]{1,0:T(8,128)(2,1)}) custom-call(bf16[1536,768]{1,0:T(8,128)(2,1)} %bitcast.39, bf16[1536,768]{1,0:T(8,128)(2,1)} %bitcast.40), custom_call_target="tpu_custom_call" | custom-call | flops 1811939328 | bytes 9437184 | tf_op jit(solution)/shard_map/pallas_call | solution.py:111
  108.2 28.5 %shard_map.139 = (bf16[1024,3200]{1,0:T(8,128)(2,1)}, bf16[1536,2048]{1,0:T(8,128)(2,1)}, bf16[1536,768]{1,0:T(8,128)(2,1)}, bf16[1536,768]{1,0:T(8,128)(2,1)}, bf16[1536,768]{1,0:T(8,128)(2,1)}) custom-call(bf16[1024,3072]{1,0:T(8,128)(2,1)} %bitcast.4.packed_ref, bf16[1536,768]{1,0:T(8,128)(2,1)} %get-tuple-element.16.a_ref, ...), custom_call_target="tpu_custom_call" | custom-call | flops 14495514624 | bytes 18874368 | tf_op jit(solution)/shard_map/pallas_call | solution.py:215
  136.8 42.3 %all-to-all-done.1 = bf16[128,8,3072]{2,1,0:T(8,128)(2,1)} async-done(((bf16[128,8,3072]{2,1,0:T(8,128)(2,1)}), bf16[128,8,3072]{2,1,0:T(8,128)(2,1)}, u32[]{:S(2)}, u32[]{:S(2)}) %all-to-all-start.1) | async-done | bytes 6291488 | tf_op jit(solution)/shard_map/all_to_all | solution.py:336
  179.1 8.6 %all-to-all-start.2 = ((bf16[128,8,3200]{2,1,0:T(8,128)(2,1)}), bf16[128,8,3200]{2,1,0:T(8,128)(2,1)}, u32[]{:S(2)}, u32[]{:S(2)}) async-start(bf16[128,8,3200]{2,1,0:T(8,128)(2,1)} %bitcast.29), calls=%async_computation.2 | async-start | bytes 13107200 | tf_op jit(solution)/shard_map/all_to_all | solution.py:336
  187.7 0.0 copy-done.1
  187.7 0.7 copy.15.ids_ref
  188.4 0.0 copy-done.2
  188.4 0.7 copy.16.slot_ref
  189.1 0.7 copy.17.gate_ref
  189.9 6.4 %shard_map.142 = bf16[1536,2048]{1,0:T(8,128)(2,1)} custom-call(bf16[1024,3072]{1,0:T(8,128)(2,1)} %bitcast.11.packed_ref), custom_call_target="tpu_custom_call" | custom-call | flops 1073741824 | bytes 12582912 | tf_op jit(solution)/shard_map/pallas_call | solution.py:145
  196.3 0.0 copy-done.6
  196.3 0.0 slice-start
  196.3 9.7 %fusion.1 = bf16[1,2048,768]{2,1,0:T(8,128)(2,1)} fusion(bf16[1536,2048]{1,0:T(8,128)(2,1)} %shard_map.142, bf16[1536,768]{1,0:T(8,128)(2,1)S(1)} %copy-done.6), kind=kOutput, calls=%fused_computation.4 | convolution fusion | flops 4833411072 | bytes 11796480 | tf_op jit(solution)/shard_map/dot_general | solution.py:369
  206.0 0.0 copy-done.5
  206.0 6.5 %fusion = bf16[1,2048,768]{2,1,0:T(8,128)(2,1)} fusion(bf16[1536,2048]{1,0:T(8,128)(2,1)S(1)} %copy-done, bf16[1536,768]{1,0:T(8,128)(2,1)S(1)} %copy-done.5), kind=kOutput, calls=%fused_computation.3 | convolution fusion | flops 4833411072 | bytes 11796480 | tf_op jit(solution)/shard_map/dot_general | solution.py:368
  212.6 0.0 slice-done
  212.6 6.5 %fusion.2 = bf16[1,768,2048]{2,1,0:T(8,128)(2,1)} fusion(bf16[1536,768]{1,0:T(8,128)(2,1)S(1)} %copy-done.4, bf16[1536,2048]{1,0:T(8,128)(2,1)S(1)} %bitcast.43), kind=kOutput, calls=%fused_computation.5 | convolution fusion | flops 4833411072 | bytes 11796480 | tf_op jit(solution)/shard_map/dot_general | solution.py:367
  219.1 48.4 %all-to-all-done.2 = bf16[128,8,3200]{2,1,0:T(8,128)(2,1)} async-done(((bf16[128,8,3200]{2,1,0:T(8,128)(2,1)}), bf16[128,8,3200]{2,1,0:T(8,128)(2,1)}, u32[]{:S(2)}, u32[]{:S(2)}) %all-to-all-start.2) | async-done | bytes 6553632 | tf_op jit(solution)/shard_map/all_to_all | solution.py:336
  267.4 5.5 %shard_map.141 = (bf16[128,2048]{1,0:T(8,128)(2,1)}, bf16[8,128]{1,0:T(8,128)(2,1)}) custom-call(s32[128,8]{1,0:T(8,128)} %copy.15.ids_ref, s32[128,8]{1,0:T(8,128)} %copy.16.slot_ref, bf16[128,8]{1,0:T(8,128)(2,1)} %copy.17.gate_ref, bf16[1024,3200]{1,0:T(8,128)(2,1)} %bitcast.13.packed_ref), custom_call_target="tpu_custom_call" | custom-call | flops 1073741824 | bytes 6553600 | tf_op jit(solution)/shard_map/pallas_call | solution.py:316
  (13 shorter events, 0.0 us)
Async XLA Ops:
  4.9 88.7 %all-to-all-start = ((bf16[128,8,3072]{2,1,0:T(8,128)(2,1)}), bf16[128,8,3072]{2,1,0:T(8,128)(2,1)}, u32[]{:S(2)}, u32[]{:S(2)}) async-start(bf16[128,8,3072]{2,1,0:T(8,128)(2,1)} %bitcast.28), calls=%async_computation | async-start | bytes 12582912 | tf_op jit(solution)/shard_map/all_to_all | solution.py:336
  93.6 85.4 %all-to-all-start.1 = ((bf16[128,8,3072]{2,1,0:T(8,128)(2,1)}), bf16[128,8,3072]{2,1,0:T(8,128)(2,1)}, u32[]{:S(2)}, u32[]{:S(2)}) async-start(bf16[128,8,3072]{2,1,0:T(8,128)(2,1)} %bitcast.27), calls=%async_computation.1 | async-start | bytes 12582912 | tf_op jit(solution)/shard_map/all_to_all | solution.py:336
  179.1 8.6 %copy-start.1 = (s32[128,8]{0,1:T(8,128)S(1)}, s32[128,8]{0,1:T(8,128)}, u32[]{:S(2)}) copy-start(s32[128,8]{0,1:T(8,128)} %param.12) | copy-start | bytes 12292
  179.1 9.4 %copy-start.2 = (s32[128,8]{0,1:T(8,128)S(1)}, s32[128,8]{0,1:T(8,128)}, u32[]{:S(2)}) copy-start(s32[128,8]{0,1:T(8,128)} %param.13) | copy-start | bytes 12292
  179.1 10.1 %copy-start.3 = (bf16[128,8]{0,1:T(8,128)(2,1)S(1)}, bf16[128,8]{0,1:T(8,128)(2,1)}, u32[]{:S(2)}) copy-start(bf16[128,8]{0,1:T(8,128)(2,1)} %param.14) | copy-start | bytes 6148
  179.1 88.4 %all-to-all-start.2 = ((bf16[128,8,3200]{2,1,0:T(8,128)(2,1)}), bf16[128,8,3200]{2,1,0:T(8,128)(2,1)}, u32[]{:S(2)}, u32[]{:S(2)}) async-start(bf16[128,8,3200]{2,1,0:T(8,128)(2,1)} %bitcast.29), calls=%async_computation.2 | async-start | bytes 13107200 | tf_op jit(solution)/shard_map/all_to_all | solution.py:336
  189.9 6.4 %copy-start.6 = (bf16[1536,768]{1,0:T(8,128)(2,1)S(1)}, bf16[1536,768]{1,0:T(8,128)(2,1)}, u32[]{:S(2)}) copy-start(bf16[1536,768]{1,0:T(8,128)(2,1)} %get-tuple-element.24) | copy-start | bytes 7077892
  196.3 9.7 %copy-start = (bf16[1536,2048]{1,0:T(8,128)(2,1)S(1)}, bf16[1536,2048]{1,0:T(8,128)(2,1)}, u32[]{:S(2)}) copy-start(bf16[1536,2048]{1,0:T(8,128)(2,1)} %shard_map.142) | copy-start | bytes 18874372
  196.3 9.7 %copy-start.5 = (bf16[1536,768]{1,0:T(8,128)(2,1)S(1)}, bf16[1536,768]{1,0:T(8,128)(2,1)}, u32[]{:S(2)}) copy-start(bf16[1536,768]{1,0:T(8,128)(2,1)} %get-tuple-element.23) | copy-start | bytes 7077892
  196.3 16.3 %slice-start = ((s8[6291456]{0:T(1024)(128)(4,1)}), s8[4194304]{0:T(1024)(128)(4,1)S(1)}, s32[]{:S(2)}) async-start(s8[6291456]{0:T(1024)(128)(4,1)} %bitcast.42), calls=%async_computation.3 | async-start | bytes 8388608
  206.0 6.6 %slice-start.1 = ((s8[6291456]{0:T(1024)(128)(4,1)}), s8[2097152]{0:T(1024)(128)(4,1)S(1)}, s32[]{:S(2)}) async-start(s8[6291456]{0:T(1024)(128)(4,1)} %bitcast.42), calls=%async_computation.4 | async-start | bytes 4194304
  206.0 6.5 %copy-start.4 = (bf16[1536,768]{1,0:T(8,128)(2,1)S(1)}, bf16[1536,768]{1,0:T(8,128)(2,1)}, u32[]{:S(2)}) copy-start(bf16[1536,768]{1,0:T(8,128)(2,1)} %get-tuple-element.25) | copy-start | bytes 7077892

commit v5 on v4

--- a/solution.py
+++ b/solution.py
@@ -15,6 +15,7 @@
 LOAD = 256
 NT = (((1,), (1,)), ((), ()))
 VMEM_LIMIT = 56 * 1024 * 1024
+SMALL_VMEM = 20 * 1024 * 1024
 
 EXTRA = 128
 
@@ -148,7 +149,7 @@
         in_specs=[pl.BlockSpec((CHUNK, wide), lambda i: (i, 0))],
         out_specs=pl.BlockSpec((CHUNK * 3 // 2, width), lambda i: (i, 0)),
         out_shape=jax.ShapeDtypeStruct((total * 3 // 2, width), BF16),
-        compiler_params=pltpu.CompilerParams(vmem_limit_bytes=VMEM_LIMIT),
+        compiler_params=pltpu.CompilerParams(vmem_limit_bytes=SMALL_VMEM),
         cost_estimate=pl.CostEstimate(
             flops=total * CHUNK * width * 2, bytes_accessed=total * wide * 4, transcendentals=0
         ),
@@ -325,7 +326,7 @@
             pltpu.VMEM((3 * toks, total), BF16),
             pltpu.SemaphoreType.DMA((total // LOAD,)),
         ],
-        compiler_params=pltpu.CompilerParams(vmem_limit_bytes=VMEM_LIMIT),
+        compiler_params=pltpu.CompilerParams(vmem_limit_bytes=SMALL_VMEM),
         cost_estimate=pl.CostEstimate(
             flops=2 * total * toks * width * 2, bytes_accessed=total * wide * 2, transcendentals=0
         ),

time: 274 us -> 273 us (level)
  waiting for transfers between devices: 163 us -> 170 us
  matrix products: 22.7 us -> 19.5 us
  Pallas kernels: 55 us -> 52 us
    all_to_all x3, waiting for transfers between devices: 163 us -> 170 us  [exchange(): return lax.all_to_all(x, axes, split_axis=0, concat_axis=0, tiled=True)]
    dot_general x1, matrix products: 9.71 us -> 6.53 us  [body(): lax.dot_general(token_rows, preup, over_rows, preferred_element_type=F32)]
  transfers between devices with their start and end apart: 3 -> 3, of which waited for: 3 -> 3; matrix products, arithmetic and copies ran while one was open for 9% -> 7% of each run, Pallas kernels for 17% -> 16%
where the time goes in v5:
time: 273 us; the launch traced here: 272 us
  waiting for transfers between devices  170 us (62%)
  Pallas kernels  52 us (19%)
  starting transfers between devices  29.1 us (11%)
  matrix products  19.5 us (7%)
    all_to_all x3, waiting for transfers between devices, exchange(): return lax.all_to_all(x, axes, split_axis=0, concat_axis=0, tiled=True)  170 us
    all_to_all x3, starting transfers between devices, exchange(): return lax.all_to_all(x, axes, split_axis=0, concat_axis=0, tiled=True)  29.1 us
    pallas_call x1, Pallas kernels, expert(): pl.pallas_call(expert_kernel, grid=(total // CHUNK,), in_specs=[packed_sp...  28.6 us
    pallas_call x2, Pallas kernels, pack(): pl.pallas_call(functools.partial(pack_kernel, scaled), out_specs=pl.Block...  8.48 us
    dot_general x1, matrix products, body(): lax.dot_general(token_rows, pregate, over_rows, preferred_element_type=F32)  6.54 us
    dot_general x1, matrix products, body(): lax.dot_general(token_rows, preup, over_rows, preferred_element_type=F32)  6.53 us
    dot_general x1, matrix products, body(): lax.dot_general(hidden, grad_rows, over_rows, preferred_element_type=F32)  6.47 us
    pallas_call x1, Pallas kernels, sort_rows(): pl.pallas_call(sort_kernel, grid=(rows // step,), in_specs=[spec, spec],...  6 us
  transfers between devices with their start and end apart: 3, of which 3 were waited for; matrix products, arithmetic and copies ran while one was open for 7% of the time, Pallas kernels for 16%

profile of v5, /device:TPU:1, one launch (start us, length us, event | category | flops | bytes accessed | tf_op | source)
XLA Modules:
  0.0 272.2 jit_solution(14491854390164300127)
XLA Ops:
  0.6 4.2 %shard_map.137 = bf16[1024,3072]{1,0:T(8,128)(2,1)} custom-call(s32[8,128]{1,0:T(8,128)} %bitcast.30, s32[8,128]{1,0:T(8,128)} %bitcast.32, bf16[8,128]{1,0:T(8,128)(2,1)} %bitcast.34, bf16[128,2048]{1,0:T(8,128)(2,1)} %x_ref.2), custom_call_target="tpu_custom_call" | custom-call | flops 1073741824 | bytes 6291456 | tf_op jit(solution)/shard_map/pallas_call | solution.py:78
  4.9 11.9 %all-to-all-start = ((bf16[128,8,3072]{2,1,0:T(8,128)(2,1)}), bf16[128,8,3072]{2,1,0:T(8,128)(2,1)}, u32[]{:S(2)}, u32[]{:S(2)}) async-start(bf16[128,8,3072]{2,1,0:T(8,128)(2,1)} %bitcast.28), calls=%async_computation | async-start | bytes 12582912 | tf_op jit(solution)/shard_map/all_to_all | solution.py:337
  16.8 4.3 %shard_map.140 = bf16[1024,3072]{1,0:T(8,128)(2,1)} custom-call(s32[8,128]{1,0:T(8,128)} %bitcast.31, s32[8,128]{1,0:T(8,128)} %bitcast.33, bf16[8,128]{1,0:T(8,128)(2,1)} %bitcast.35, bf16[128,2048]{1,0:T(8,128)(2,1)} %x_ref.3), custom_call_target="tpu_custom_call" | custom-call | flops 1073741824 | bytes 6291456 | tf_op jit(solution)/shard_map/pallas_call | solution.py:78
  21.0 72.6 %all-to-all-done = bf16[128,8,3072]{2,1,0:T(8,128)(2,1)} async-done(((bf16[128,8,3072]{2,1,0:T(8,128)(2,1)}), bf16[128,8,3072]{2,1,0:T(8,128)(2,1)}, u32[]{:S(2)}, u32[]{:S(2)}) %all-to-all-start) | async-done | bytes 6291488 | tf_op jit(solution)/shard_map/all_to_all | solution.py:337
  93.6 8.6 %all-to-all-start.1 = ((bf16[128,8,3072]{2,1,0:T(8,128)(2,1)}), bf16[128,8,3072]{2,1,0:T(8,128)(2,1)}, u32[]{:S(2)}, u32[]{:S(2)}) async-start(bf16[128,8,3072]{2,1,0:T(8,128)(2,1)} %bitcast.27), calls=%async_computation.1 | async-start | bytes 12582912 | tf_op jit(solution)/shard_map/all_to_all | solution.py:337
  102.2 6.0 %shard_map.138 = (bf16[1536,768]{1,0:T(8,128)(2,1)}, bf16[1536,768]{1,0:T(8,128)(2,1)}) custom-call(bf16[1536,768]{1,0:T(8,128)(2,1)} %bitcast.39, bf16[1536,768]{1,0:T(8,128)(2,1)} %bitcast.40), custom_call_target="tpu_custom_call" | custom-call | flops 1811939328 | bytes 9437184 | tf_op jit(solution)/shard_map/pallas_call | solution.py:112
  108.2 28.6 %shard_map.139 = (bf16[1024,3200]{1,0:T(8,128)(2,1)}, bf16[1536,2048]{1,0:T(8,128)(2,1)}, bf16[1536,768]{1,0:T(8,128)(2,1)}, bf16[1536,768]{1,0:T(8,128)(2,1)}, bf16[1536,768]{1,0:T(8,128)(2,1)}) custom-call(bf16[1024,3072]{1,0:T(8,128)(2,1)} %bitcast.4.packed_ref, bf16[1536,768]{1,0:T(8,128)(2,1)} %get-tuple-element.16.a_ref, ...), custom_call_target="tpu_custom_call" | custom-call | flops 14495514624 | bytes 18874368 | tf_op jit(solution)/shard_map/pallas_call | solution.py:216
  136.8 42.3 %all-to-all-done.1 = bf16[128,8,3072]{2,1,0:T(8,128)(2,1)} async-done(((bf16[128,8,3072]{2,1,0:T(8,128)(2,1)}), bf16[128,8,3072]{2,1,0:T(8,128)(2,1)}, u32[]{:S(2)}, u32[]{:S(2)}) %all-to-all-start.1) | async-done | bytes 6291488 | tf_op jit(solution)/shard_map/all_to_all | solution.py:337
  179.1 8.6 %all-to-all-start.2 = ((bf16[128,8,3200]{2,1,0:T(8,128)(2,1)}), bf16[128,8,3200]{2,1,0:T(8,128)(2,1)}, u32[]{:S(2)}, u32[]{:S(2)}) async-start(bf16[128,8,3200]{2,1,0:T(8,128)(2,1)} %bitcast.29), calls=%async_computation.2 | async-start | bytes 13107200 | tf_op jit(solution)/shard_map/all_to_all | solution.py:337
  187.7 0.0 copy-done
  187.7 0.1 copy.15.ids_ref
  187.8 0.0 copy-done.1
  187.8 0.1 copy.16.slot_ref
  187.9 0.0 copy-done.2
  187.9 0.1 copy.17.gate_ref
  188.0 4.3 %shard_map.142 = bf16[1536,2048]{1,0:T(8,128)(2,1)S(1)} custom-call(bf16[1024,3072]{1,0:T(8,128)(2,1)} %bitcast.11.packed_ref), custom_call_target="tpu_custom_call" | custom-call | flops 1073741824 | bytes 12582912 | tf_op jit(solution)/shard_map/pallas_call | solution.py:146
  192.4 0.0 copy-start.4
  192.4 0.0 slice-start
  192.4 6.5 %fusion.1 = bf16[1,2048,768]{2,1,0:T(8,128)(2,1)} fusion(bf16[1536,2048]{1,0:T(8,128)(2,1)S(1)} %shard_map.142, bf16[1536,768]{1,0:T(8,128)(2,1)S(1)} %copy-done.5), kind=kOutput, calls=%fused_computation.4 | convolution fusion | flops 4833411072 | bytes 11796480 | tf_op jit(solution)/shard_map/dot_general | solution.py:370
  198.9 0.0 copy-done.4
  198.9 6.5 %fusion = bf16[1,2048,768]{2,1,0:T(8,128)(2,1)} fusion(bf16[1536,2048]{1,0:T(8,128)(2,1)S(1)} %shard_map.142, bf16[1536,768]{1,0:T(8,128)(2,1)S(1)} %copy-done.4), kind=kOutput, calls=%fused_computation.3 | convolution fusion | flops 4833411072 | bytes 11796480 | tf_op jit(solution)/shard_map/dot_general | solution.py:369
  205.5 6.5 %fusion.2 = bf16[1,768,2048]{2,1,0:T(8,128)(2,1)} fusion(bf16[1536,768]{1,0:T(8,128)(2,1)S(1)} %copy-done.3, bf16[1536,2048]{1,0:T(8,128)(2,1)S(1)} %bitcast.43), kind=kOutput, calls=%fused_computation.5 | convolution fusion | flops 4833411072 | bytes 11796480 | tf_op jit(solution)/shard_map/dot_general | solution.py:368
  212.0 55.5 %all-to-all-done.2 = bf16[128,8,3200]{2,1,0:T(8,128)(2,1)} async-done(((bf16[128,8,3200]{2,1,0:T(8,128)(2,1)}), bf16[128,8,3200]{2,1,0:T(8,128)(2,1)}, u32[]{:S(2)}, u32[]{:S(2)}) %all-to-all-start.2) | async-done | bytes 6553632 | tf_op jit(solution)/shard_map/all_to_all | solution.py:337
  267.4 4.6 %shard_map.141 = (bf16[128,2048]{1,0:T(8,128)(2,1)}, bf16[8,128]{1,0:T(8,128)(2,1)}) custom-call(s32[128,8]{1,0:T(8,128)S(1)} %copy.15.ids_ref, s32[128,8]{1,0:T(8,128)S(1)} %copy.16.slot_ref, bf16[128,8]{1,0:T(8,128)(2,1)S(1)} %copy.17.gate_ref, bf16[1024,3200]{1,0:T(8,128)(2,1)} %bitcast.13.packed_ref), custom_call_target="tpu_custom_call" | custom-call | flops 1073741824 | bytes 6553600 | tf_op jit(solution)/shard_map/pallas_call | solution.py:317
  (11 shorter events, 0.0 us)
Async XLA Ops:
  4.9 88.7 %all-to-all-start = ((bf16[128,8,3072]{2,1,0:T(8,128)(2,1)}), bf16[128,8,3072]{2,1,0:T(8,128)(2,1)}, u32[]{:S(2)}, u32[]{:S(2)}) async-start(bf16[128,8,3072]{2,1,0:T(8,128)(2,1)} %bitcast.28), calls=%async_computation | async-start | bytes 12582912 | tf_op jit(solution)/shard_map/all_to_all | solution.py:337
  93.6 85.4 %all-to-all-start.1 = ((bf16[128,8,3072]{2,1,0:T(8,128)(2,1)}), bf16[128,8,3072]{2,1,0:T(8,128)(2,1)}, u32[]{:S(2)}, u32[]{:S(2)}) async-start(bf16[128,8,3072]{2,1,0:T(8,128)(2,1)} %bitcast.27), calls=%async_computation.1 | async-start | bytes 12582912 | tf_op jit(solution)/shard_map/all_to_all | solution.py:337
  179.1 8.6 %copy-start = (s32[128,8]{0,1:T(8,128)S(1)}, s32[128,8]{0,1:T(8,128)}, u32[]{:S(2)}) copy-start(s32[128,8]{0,1:T(8,128)} %param.12) | copy-start | bytes 12292
  179.1 8.7 %copy-start.1 = (s32[128,8]{0,1:T(8,128)S(1)}, s32[128,8]{0,1:T(8,128)}, u32[]{:S(2)}) copy-start(s32[128,8]{0,1:T(8,128)} %param.13) | copy-start | bytes 12292
  179.1 8.8 %copy-start.2 = (bf16[128,8]{0,1:T(8,128)(2,1)S(1)}, bf16[128,8]{0,1:T(8,128)(2,1)}, u32[]{:S(2)}) copy-start(bf16[128,8]{0,1:T(8,128)(2,1)} %param.14) | copy-start | bytes 6148
  179.1 88.4 %all-to-all-start.2 = ((bf16[128,8,3200]{2,1,0:T(8,128)(2,1)}), bf16[128,8,3200]{2,1,0:T(8,128)(2,1)}, u32[]{:S(2)}, u32[]{:S(2)}) async-start(bf16[128,8,3200]{2,1,0:T(8,128)(2,1)} %bitcast.29), calls=%async_computation.2 | async-start | bytes 13107200 | tf_op jit(solution)/shard_map/all_to_all | solution.py:337
  188.0 4.3 %copy-start.5 = (bf16[1536,768]{1,0:T(8,128)(2,1)S(1)}, bf16[1536,768]{1,0:T(8,128)(2,1)}, u32[]{:S(2)}) copy-start(bf16[1536,768]{1,0:T(8,128)(2,1)} %get-tuple-element.24) | copy-start | bytes 7077892
  192.4 6.6 %copy-start.4 = (bf16[1536,768]{1,0:T(8,128)(2,1)S(1)}, bf16[1536,768]{1,0:T(8,128)(2,1)}, u32[]{:S(2)}) copy-start(bf16[1536,768]{1,0:T(8,128)(2,1)} %get-tuple-element.23) | copy-start | bytes 7077892
  192.4 13.1 %slice-start = ((s8[6291456]{0:T(1024)(128)(4,1)}), s8[4194304]{0:T(1024)(128)(4,1)S(1)}, s32[]{:S(2)}) async-start(s8[6291456]{0:T(1024)(128)(4,1)} %bitcast.42), calls=%async_computation.3 | async-start | bytes 8388608
  198.9 6.5 %slice-start.1 = ((s8[6291456]{0:T(1024)(128)(4,1)}), s8[2097152]{0:T(1024)(128)(4,1)S(1)}, s32[]{:S(2)}) async-start(s8[6291456]{0:T(1024)(128)(4,1)} %bitcast.42), calls=%async_computation.4 | async-start | bytes 4194304
  198.9 6.5 %copy-start.3 = (bf16[1536,768]{1,0:T(8,128)(2,1)S(1)}, bf16[1536,768]{1,0:T(8,128)(2,1)}, u32[]{:S(2)}) copy-start(bf16[1536,768]{1,0:T(8,128)(2,1)} %get-tuple-element.25) | copy-start | bytes 7077892

commit v6 on v5

--- a/solution.py
+++ b/solution.py
@@ -12,7 +12,7 @@
 AXES = ("group", "member")
 CHUNK = 256
 BLOCK = 128
-LOAD = 256
+LOAD = 512
 NT = (((1,), (1,)), ((), ()))
 VMEM_LIMIT = 56 * 1024 * 1024
 SMALL_VMEM = 20 * 1024 * 1024

time: 273 us -> 273 us (level)
  no operation moved by 1% of the time
where the time goes in v6:
time: 273 us; the launch traced here: 272 us
  waiting for transfers between devices  170 us (62%)
  Pallas kernels  52.1 us (19%)
  starting transfers between devices  29.1 us (11%)
  matrix products  19.5 us (7%)
    all_to_all x3, waiting for transfers between devices, exchange(): return lax.all_to_all(x, axes, split_axis=0, concat_axis=0, tiled=True)  170 us
    all_to_all x3, starting transfers between devices, exchange(): return lax.all_to_all(x, axes, split_axis=0, concat_axis=0, tiled=True)  29.1 us
    pallas_call x1, Pallas kernels, expert(): pl.pallas_call(expert_kernel, grid=(total // CHUNK,), in_specs=[packed_sp...  28.6 us
    pallas_call x2, Pallas kernels, pack(): pl.pallas_call(functools.partial(pack_kernel, scaled), out_specs=pl.Block...  8.48 us
    dot_general x1, matrix products, body(): lax.dot_general(token_rows, pregate, over_rows, preferred_element_type=F32)  6.54 us
    dot_general x1, matrix products, body(): lax.dot_general(token_rows, preup, over_rows, preferred_element_type=F32)  6.53 us
    dot_general x1, matrix products, body(): lax.dot_general(hidden, grad_rows, over_rows, preferred_element_type=F32)  6.47 us
    pallas_call x1, Pallas kernels, sort_rows(): pl.pallas_call(sort_kernel, grid=(rows // step,), in_specs=[spec, spec],...  6 us
  transfers between devices with their start and end apart: 3, of which 3 were waited for; matrix products, arithmetic and copies ran while one was open for 7% of the time, Pallas kernels for 16%

profile of v6, /device:TPU:1, one launch (start us, length us, event | category | flops | bytes accessed | tf_op | source)
XLA Modules:
  0.0 272.3 jit_solution(13003030337977402505)
XLA Ops:
  0.6 4.2 %shard_map.137 = bf16[1024,3072]{1,0:T(8,128)(2,1)} custom-call(s32[8,128]{1,0:T(8,128)} %bitcast.30, s32[8,128]{1,0:T(8,128)} %bitcast.32, bf16[8,128]{1,0:T(8,128)(2,1)} %bitcast.34, bf16[128,2048]{1,0:T(8,128)(2,1)} %x_ref.2), custom_call_target="tpu_custom_call" | custom-call | flops 1073741824 | bytes 6291456 | tf_op jit(solution)/shard_map/pallas_call | solution.py:78
  4.9 11.9 %all-to-all-start = ((bf16[128,8,3072]{2,1,0:T(8,128)(2,1)}), bf16[128,8,3072]{2,1,0:T(8,128)(2,1)}, u32[]{:S(2)}, u32[]{:S(2)}) async-start(bf16[128,8,3072]{2,1,0:T(8,128)(2,1)} %bitcast.28), calls=%async_computation | async-start | bytes 12582912 | tf_op jit(solution)/shard_map/all_to_all | solution.py:337
  16.8 4.3 %shard_map.140 = bf16[1024,3072]{1,0:T(8,128)(2,1)} custom-call(s32[8,128]{1,0:T(8,128)} %bitcast.31, s32[8,128]{1,0:T(8,128)} %bitcast.33, bf16[8,128]{1,0:T(8,128)(2,1)} %bitcast.35, bf16[128,2048]{1,0:T(8,128)(2,1)} %x_ref.3), custom_call_target="tpu_custom_call" | custom-call | flops 1073741824 | bytes 6291456 | tf_op jit(solution)/shard_map/pallas_call | solution.py:78
  21.0 72.6 %all-to-all-done = bf16[128,8,3072]{2,1,0:T(8,128)(2,1)} async-done(((bf16[128,8,3072]{2,1,0:T(8,128)(2,1)}), bf16[128,8,3072]{2,1,0:T(8,128)(2,1)}, u32[]{:S(2)}, u32[]{:S(2)}) %all-to-all-start) | async-done | bytes 6291488 | tf_op jit(solution)/shard_map/all_to_all | solution.py:337
  93.6 8.6 %all-to-all-start.1 = ((bf16[128,8,3072]{2,1,0:T(8,128)(2,1)}), bf16[128,8,3072]{2,1,0:T(8,128)(2,1)}, u32[]{:S(2)}, u32[]{:S(2)}) async-start(bf16[128,8,3072]{2,1,0:T(8,128)(2,1)} %bitcast.27), calls=%async_computation.1 | async-start | bytes 12582912 | tf_op jit(solution)/shard_map/all_to_all | solution.py:337
  102.2 6.0 %shard_map.138 = (bf16[1536,768]{1,0:T(8,128)(2,1)}, bf16[1536,768]{1,0:T(8,128)(2,1)}) custom-call(bf16[1536,768]{1,0:T(8,128)(2,1)} %bitcast.39, bf16[1536,768]{1,0:T(8,128)(2,1)} %bitcast.40), custom_call_target="tpu_custom_call" | custom-call | flops 1811939328 | bytes 9437184 | tf_op jit(solution)/shard_map/pallas_call | solution.py:112
  108.2 28.6 %shard_map.139 = (bf16[1024,3200]{1,0:T(8,128)(2,1)}, bf16[1536,2048]{1,0:T(8,128)(2,1)}, bf16[1536,768]{1,0:T(8,128)(2,1)}, bf16[1536,768]{1,0:T(8,128)(2,1)}, bf16[1536,768]{1,0:T(8,128)(2,1)}) custom-call(bf16[1024,3072]{1,0:T(8,128)(2,1)} %bitcast.4.packed_ref, bf16[1536,768]{1,0:T(8,128)(2,1)} %get-tuple-element.16.a_ref, ...), custom_call_target="tpu_custom_call" | custom-call | flops 14495514624 | bytes 18874368 | tf_op jit(solution)/shard_map/pallas_call | solution.py:216
  136.8 42.3 %all-to-all-done.1 = bf16[128,8,3072]{2,1,0:T(8,128)(2,1)} async-done(((bf16[128,8,3072]{2,1,0:T(8,128)(2,1)}), bf16[128,8,3072]{2,1,0:T(8,128)(2,1)}, u32[]{:S(2)}, u32[]{:S(2)}) %all-to-all-start.1) | async-done | bytes 6291488 | tf_op jit(solution)/shard_map/all_to_all | solution.py:337
  179.1 8.6 %all-to-all-start.2 = ((bf16[128,8,3200]{2,1,0:T(8,128)(2,1)}), bf16[128,8,3200]{2,1,0:T(8,128)(2,1)}, u32[]{:S(2)}, u32[]{:S(2)}) async-start(bf16[128,8,3200]{2,1,0:T(8,128)(2,1)} %bitcast.29), calls=%async_computation.2 | async-start | bytes 13107200 | tf_op jit(solution)/shard_map/all_to_all | solution.py:337
  187.7 0.0 copy-done
  187.7 0.1 copy.15.ids_ref
  187.8 0.0 copy-done.1
  187.8 0.1 copy.16.slot_ref
  187.9 0.0 copy-done.2
  187.9 0.1 copy.17.gate_ref
  188.0 4.3 %shard_map.142 = bf16[1536,2048]{1,0:T(8,128)(2,1)S(1)} custom-call(bf16[1024,3072]{1,0:T(8,128)(2,1)} %bitcast.11.packed_ref), custom_call_target="tpu_custom_call" | custom-call | flops 1073741824 | bytes 12582912 | tf_op jit(solution)/shard_map/pallas_call | solution.py:146
  192.4 0.0 copy-start.4
  192.4 0.0 slice-start
  192.4 6.5 %fusion.1 = bf16[1,2048,768]{2,1,0:T(8,128)(2,1)} fusion(bf16[1536,2048]{1,0:T(8,128)(2,1)S(1)} %shard_map.142, bf16[1536,768]{1,0:T(8,128)(2,1)S(1)} %copy-done.5), kind=kOutput, calls=%fused_computation.4 | convolution fusion | flops 4833411072 | bytes 11796480 | tf_op jit(solution)/shard_map/dot_general | solution.py:370
  198.9 0.0 copy-done.4
  198.9 6.5 %fusion = bf16[1,2048,768]{2,1,0:T(8,128)(2,1)} fusion(bf16[1536,2048]{1,0:T(8,128)(2,1)S(1)} %shard_map.142, bf16[1536,768]{1,0:T(8,128)(2,1)S(1)} %copy-done.4), kind=kOutput, calls=%fused_computation.3 | convolution fusion | flops 4833411072 | bytes 11796480 | tf_op jit(solution)/shard_map/dot_general | solution.py:369
  205.5 6.5 %fusion.2 = bf16[1,768,2048]{2,1,0:T(8,128)(2,1)} fusion(bf16[1536,768]{1,0:T(8,128)(2,1)S(1)} %copy-done.3, bf16[1536,2048]{1,0:T(8,128)(2,1)S(1)} %bitcast.43), kind=kOutput, calls=%fused_computation.5 | convolution fusion | flops 4833411072 | bytes 11796480 | tf_op jit(solution)/shard_map/dot_general | solution.py:368
  212.0 55.5 %all-to-all-done.2 = bf16[128,8,3200]{2,1,0:T(8,128)(2,1)} async-done(((bf16[128,8,3200]{2,1,0:T(8,128)(2,1)}), bf16[128,8,3200]{2,1,0:T(8,128)(2,1)}, u32[]{:S(2)}, u32[]{:S(2)}) %all-to-all-start.2) | async-done | bytes 6553632 | tf_op jit(solution)/shard_map/all_to_all | solution.py:337
  267.4 4.7 %shard_map.141 = (bf16[128,2048]{1,0:T(8,128)(2,1)}, bf16[8,128]{1,0:T(8,128)(2,1)}) custom-call(s32[128,8]{1,0:T(8,128)S(1)} %copy.15.ids_ref, s32[128,8]{1,0:T(8,128)S(1)} %copy.16.slot_ref, bf16[128,8]{1,0:T(8,128)(2,1)S(1)} %copy.17.gate_ref, bf16[1024,3200]{1,0:T(8,128)(2,1)} %bitcast.13.packed_ref), custom_call_target="tpu_custom_call" | custom-call | flops 1073741824 | bytes 6553600 | tf_op jit(solution)/shard_map/pallas_call | solution.py:317
  (11 shorter events, 0.0 us)
Async XLA Ops:
  4.9 88.7 %all-to-all-start = ((bf16[128,8,3072]{2,1,0:T(8,128)(2,1)}), bf16[128,8,3072]{2,1,0:T(8,128)(2,1)}, u32[]{:S(2)}, u32[]{:S(2)}) async-start(bf16[128,8,3072]{2,1,0:T(8,128)(2,1)} %bitcast.28), calls=%async_computation | async-start | bytes 12582912 | tf_op jit(solution)/shard_map/all_to_all | solution.py:337
  93.6 85.4 %all-to-all-start.1 = ((bf16[128,8,3072]{2,1,0:T(8,128)(2,1)}), bf16[128,8,3072]{2,1,0:T(8,128)(2,1)}, u32[]{:S(2)}, u32[]{:S(2)}) async-start(bf16[128,8,3072]{2,1,0:T(8,128)(2,1)} %bitcast.27), calls=%async_computation.1 | async-start | bytes 12582912 | tf_op jit(solution)/shard_map/all_to_all | solution.py:337
  179.1 8.6 %copy-start = (s32[128,8]{0,1:T(8,128)S(1)}, s32[128,8]{0,1:T(8,128)}, u32[]{:S(2)}) copy-start(s32[128,8]{0,1:T(8,128)} %param.12) | copy-start | bytes 12292
  179.1 8.7 %copy-start.1 = (s32[128,8]{0,1:T(8,128)S(1)}, s32[128,8]{0,1:T(8,128)}, u32[]{:S(2)}) copy-start(s32[128,8]{0,1:T(8,128)} %param.13) | copy-start | bytes 12292
  179.1 8.8 %copy-start.2 = (bf16[128,8]{0,1:T(8,128)(2,1)S(1)}, bf16[128,8]{0,1:T(8,128)(2,1)}, u32[]{:S(2)}) copy-start(bf16[128,8]{0,1:T(8,128)(2,1)} %param.14) | copy-start | bytes 6148
  179.1 88.4 %all-to-all-start.2 = ((bf16[128,8,3200]{2,1,0:T(8,128)(2,1)}), bf16[128,8,3200]{2,1,0:T(8,128)(2,1)}, u32[]{:S(2)}, u32[]{:S(2)}) async-start(bf16[128,8,3200]{2,1,0:T(8,128)(2,1)} %bitcast.29), calls=%async_computation.2 | async-start | bytes 13107200 | tf_op jit(solution)/shard_map/all_to_all | solution.py:337
  188.0 4.3 %copy-start.5 = (bf16[1536,768]{1,0:T(8,128)(2,1)S(1)}, bf16[1536,768]{1,0:T(8,128)(2,1)}, u32[]{:S(2)}) copy-start(bf16[1536,768]{1,0:T(8,128)(2,1)} %get-tuple-element.24) | copy-start | bytes 7077892
  192.4 6.6 %copy-start.4 = (bf16[1536,768]{1,0:T(8,128)(2,1)S(1)}, bf16[1536,768]{1,0:T(8,128)(2,1)}, u32[]{:S(2)}) copy-start(bf16[1536,768]{1,0:T(8,128)(2,1)} %get-tuple-element.23) | copy-start | bytes 7077892
  192.4 13.1 %slice-start = ((s8[6291456]{0:T(1024)(128)(4,1)}), s8[4194304]{0:T(1024)(128)(4,1)S(1)}, s32[]{:S(2)}) async-start(s8[6291456]{0:T(1024)(128)(4,1)} %bitcast.42), calls=%async_computation.3 | async-start | bytes 8388608
  198.9 6.5 %slice-start.1 = ((s8[6291456]{0:T(1024)(128)(4,1)}), s8[2097152]{0:T(1024)(128)(4,1)S(1)}, s32[]{:S(2)}) async-start(s8[6291456]{0:T(1024)(128)(4,1)} %bitcast.42), calls=%async_computation.4 | async-start | bytes 4194304
  198.9 6.5 %copy-start.3 = (bf16[1536,768]{1,0:T(8,128)(2,1)S(1)}, bf16[1536,768]{1,0:T(8,128)(2,1)}, u32[]{:S(2)}) copy-start(bf16[1536,768]{1,0:T(8,128)(2,1)} %get-tuple-element.25) | copy-start | bytes 7077892
